TPU v7x, 32 devices: a whole 2x2x4 slice. The times are simulated.
32 devices in a mesh: dp: 16 (over z, x, core), mp: 2 (over y).
Axes of the slice: x: 2, y: 2, z: 4, core: 2. Of those that a mesh axis runs over, the one named last changes fastest.
Arguments:
- resp_q: bfloat16 [16, 128, 8192], P('dp', None, 'mp'), may hold values from -12 to 12, as said below
- resp_kv: bfloat16 [2, 16, 128, 1024], P(None, 'dp', None, 'mp'), may hold values from -4 to 4
- d_out: bfloat16 [16, 128, 8192], P('dp', None, 'mp'), may hold values from -6 to 6
- lengths: int32 [16], P('dp'), may hold values from 1 to 128, 1536 in all
- fork: int32 [16], replicated, may hold values from 0 to 31
- page_table: int32 [32, 8], replicated, may hold values from 0 to 255, as said below
- pool_pages: bfloat16 [256, 2, 16, 1024], P(('dp', 'mp')), may hold values from -4 to 4
- pool_scales: bfloat16 [256, 2, 8], P(('dp', 'mp')), may hold values from 0.29882812 to 3
Outputs:
- d_query: bfloat16 [16, 128, 8192], P('dp', None, 'mp')
- d_resp_kv: bfloat16 [2, 16, 128, 1024], P(None, 'dp', None, 'mp')
- d_pool: float32 [256, 2, 16, 1024], P(('dp', 'mp'))
Inputs may be any that keep to these rules, and one draw needn't show every extreme that they name: `page_table`: every pool page is named exactly once. Pool page g lies on dp index g // 16, and the 8 pages of one prompt lie on 8 different dp indices. `resp_q`: query entries. On some rows, some query heads may be a multiple between 1.5 and 3 of a key of the same response, so that scores can reach several hundred.
All inputs are finite; a program needn't handle non-finite values. No bound on the sum of `lengths` on one device may be relied on, other than what follows from the above.
Results may differ from a plain program's by a relative error of at most 0.012.
Values may be sent and summed in bfloat16 or wider, within the bound.
A program may use at most 64 MiB of HBM per device.

v0:
```python
import jax
import jax.numpy as jnp
from jax import lax
from jax.sharding import PartitionSpec as P

DH = 128


def dequantize(stored, factors):
    heads = factors.shape[-1]
    head_width = stored.shape[-1] // heads
    shaped = stored.astype(jnp.float32).reshape(
        stored.shape[0], 2, stored.shape[2], heads, head_width
    )
    scaled = shaped * factors.astype(jnp.float32).reshape(stored.shape[0], 2, 1, heads, 1)
    return scaled.astype(jnp.bfloat16).reshape(stored.shape)


def per_device(resp_q, resp_kv, d_out, lengths, fork, page_table, pool_pages, pool_scales):
    dp_size = lax.axis_size("dp")
    mp_size = lax.axis_size("mp")
    my_dp = lax.axis_index("dp")
    pool_dev = pool_pages.shape[0]
    heads_kv = pool_scales.shape[-1]
    kv_dev = heads_kv // mp_size
    page_rows = pool_pages.shape[2]
    pages_prompt = page_table.shape[1]
    prompt_len = pages_prompt * page_rows
    resp_len = resp_q.shape[1]
    total = prompt_len + resp_len
    group_rows = mp_size * pool_dev
    inv_root = 1.0 / DH**0.5
    regrouped, regscales = (
        lax.all_to_all(pool_pages, "mp", split_axis=3, concat_axis=0, tiled=True),
        lax.all_to_all(
            pool_scales.reshape(pool_dev, 2, 1, heads_kv),
            "mp",
            split_axis=3,
            concat_axis=0,
            tiled=True,
        ),
    )
    wanted = jnp.take(page_table, fork, axis=0)
    on_device = wanted // group_rows == my_dp
    send_rows = jnp.sum(jnp.where(on_device, wanted % group_rows, 0), axis=1)
    has_page = jnp.any(on_device, axis=1)
    my_pages = jnp.take(wanted, my_dp, axis=0)
    sources = my_pages // group_rows
    arrived, arrived_scales = (
        lax.all_to_all(
            jnp.take(regrouped, send_rows, axis=0), "dp", split_axis=0, concat_axis=0, tiled=True
        ),
        lax.all_to_all(
            jnp.take(regscales, send_rows, axis=0), "dp", split_axis=0, concat_axis=0, tiled=True
        ),
    )
    prompt_pages = dequantize(
        jnp.take(arrived, sources, axis=0), jnp.take(arrived_scales, sources, axis=0)
    )
    key_all = jnp.concatenate(
        [prompt_pages[:, 0].reshape(prompt_len, kv_dev * DH), resp_kv[0, 0]], 0
    )
    value_all = jnp.concatenate(
        [prompt_pages[:, 1].reshape(prompt_len, kv_dev * DH), resp_kv[1, 0]], 0
    )
    key_heads = key_all.reshape(total, kv_dev, DH).transpose(1, 0, 2)
    value_heads = value_all.reshape(total, kv_dev, DH).transpose(1, 0, 2)
    heads_q_dev = resp_q.shape[2] // DH
    group_size = heads_q_dev // kv_dev
    blocks = heads_q_dev // 2
    rows_live = jnp.arange(resp_len) < lengths[0]
    grad_masked = jnp.where(rows_live[:, None], d_out[0], jnp.zeros_like(d_out[0]))
    query_blocks = (
        resp_q[0]
        .reshape(resp_len, blocks, 2, DH)
        .transpose(1, 2, 0, 3)
        .reshape(blocks, 2 * resp_len, DH)
    )
    grad_blocks = (
        grad_masked.reshape(resp_len, blocks, 2, DH)
        .transpose(1, 2, 0, 3)
        .reshape(blocks, 2 * resp_len, DH)
    )
    kv_index = jnp.arange(blocks) * 2 // group_size
    positions = jnp.tile(jnp.arange(resp_len), 2)
    key_cols = jnp.arange(total)
    allowed = (key_cols[None, :] < prompt_len) | (
        key_cols[None, :] - prompt_len <= positions[:, None]
    )
    across = (((1,), (1,)), ((), ()))
    down = (((0,), (0,)), ((), ()))

    def block_step(block_items):
        q_rows, g_rows, kv_slot = block_items
        k_head = key_heads[kv_slot]
        v_head = value_heads[kv_slot]
        scores = (
            lax.dot_general(q_rows, k_head, across, preferred_element_type=jnp.float32) * inv_root
        )
        scores = jnp.where(allowed, scores, -1e30)
        row_max = jnp.max(scores, axis=-1, keepdims=True)
        exp_scores = jnp.exp(scores - row_max)
        weights = exp_scores / jnp.sum(exp_scores, axis=-1, keepdims=True)
        weights_b = weights.astype(jnp.bfloat16)
        attn_out = jnp.dot(weights_b, v_head, preferred_element_type=jnp.float32)
        row_delta = jnp.sum(g_rows.astype(jnp.float32) * attn_out, axis=-1)
        grad_weights = lax.dot_general(g_rows, v_head, across, preferred_element_type=jnp.float32)
        grad_scores = (weights * (grad_weights - row_delta[:, None])).astype(jnp.bfloat16)
        grad_query = (
            jnp.dot(grad_scores, k_head, preferred_element_type=jnp.float32) * inv_root
        ).astype(jnp.bfloat16)
        grad_keys = (
            lax.dot_general(grad_scores, q_rows, down, preferred_element_type=jnp.float32)
            * inv_root
        )
        grad_values = lax.dot_general(weights_b, g_rows, down, preferred_element_type=jnp.float32)
        return (grad_query, grad_keys, grad_values)

    query_parts, key_parts, value_parts = lax.map(block_step, (query_blocks, grad_blocks, kv_index))
    key_sum = key_parts.reshape(kv_dev, group_size // 2, total, DH).sum(axis=1)
    value_sum = value_parts.reshape(kv_dev, group_size // 2, total, DH).sum(axis=1)
    d_query = (
        query_parts.reshape(blocks, 2, resp_len, DH)
        .transpose(2, 0, 1, 3)
        .reshape(1, resp_len, heads_q_dev * DH)
    )
    own_grads = jnp.stack([key_sum[:, prompt_len:], value_sum[:, prompt_len:]])
    own_grads = (
        own_grads.transpose(0, 2, 1, 3).reshape(2, 1, resp_len, kv_dev * DH).astype(jnp.bfloat16)
    )
    prompt_grad = jnp.stack([key_sum[:, :prompt_len], value_sum[:, :prompt_len]])
    prompt_grad = prompt_grad.reshape(2, kv_dev, pages_prompt, page_rows, DH).transpose(
        2, 0, 3, 1, 4
    )
    prompt_grad = prompt_grad.reshape(pages_prompt, 2, page_rows, kv_dev * DH)
    buffer = (
        jnp.zeros((dp_size, 2, page_rows, kv_dev * DH), jnp.float32).at[sources].set(prompt_grad)
    )
    returned = lax.all_to_all(buffer, "dp", split_axis=0, concat_axis=0, tiled=True)
    select = ((send_rows[:, None] == jnp.arange(group_rows)[None, :]) & has_page[:, None]).astype(
        jnp.float32
    )
    summed = jnp.einsum("hn,hxyz->nxyz", select, returned, precision=lax.Precision.HIGHEST)
    restored = lax.all_to_all(summed, "mp", split_axis=0, concat_axis=3, tiled=True)
    return (d_query, own_grads, restored)


def solution(mesh):
    return jax.shard_map(
        per_device,
        mesh=mesh,
        in_specs=(
            P("dp", None, "mp"),
            P(None, "dp", None, "mp"),
            P("dp", None, "mp"),
            P("dp"),
            P(),
            P(),
            P(("dp", "mp"), None, None, None),
            P(("dp", "mp"), None, None),
        ),
        out_specs=(
            P("dp", None, "mp"),
            P(None, "dp", None, "mp"),
            P(("dp", "mp"), None, None, None),
        ),
        check_vma=False,
    )
```

profile of v0, /device:TPU:0, one launch (start us, length us, event | category | flops | bytes accessed | tf_op | source)
XLA Modules:
  0.0 280.1 jit_solution(951982185275311733)
XLA Ops:
  2.0 4.2 %all-to-all-start.2 = ((bf16[8,2,1,8]{0,1,2,3:T(2,128)(2,1)}), bf16[8,2,1,8]{0,1,2,3:T(2,128)(2,1)S(1)}, u32[]{:S(2)}, u32[]{:S(2)}) async-start(bf16[8,2,1,8]{0,1,2,3:T(2,128)(2,1)} %copy.100), calls=%async_computation.2 | async-start | bytes 8192 | tf_op jit(solution)/shard_map/all_to_all | solution.py:35
  9.2 5.8 %copy.96 = bf16[8,2,16,1024]{2,0,1,3:T(8,128)(2,1)} copy(bf16[8,2,16,1024]{3,2,1,0:T(8,128)(2,1)} %param.16) | data formatting | bytes 1048576 | tf_op args[6]
  15.9 3.1 %copy.110 = bf16[128,16,2,128]{0,2,3,1:T(2,128)(2,1)S(1)} copy(bf16[128,16,2,128]{3,2,1,0:T(2,128)(2,1)S(1)} %squeeze.26) | data formatting | bytes 2097152 | tf_op jit(solution)/shard_map/squeeze | solution.py:72
  20.5 6.6 %reshape.296 = bf16[2,2,65536]{2,1,0:T(2,128)(2,1)} reshape(bf16[1024,2,8,16]{3,2,1,0:T(8,128)(2,1)} %bitcast.159) | data formatting | bytes 1048576
  27.1 3.6 %all-to-all-start = ((bf16[2,2,65536]{2,1,0:T(2,128)(2,1)}), bf16[2,2,65536]{2,1,0:T(2,128)(2,1)S(1)}, u32[]{:S(2)}, u32[]{:S(2)}) async-start(bf16[2,2,65536]{2,1,0:T(2,128)(2,1)} %reshape.296), calls=%async_computation | async-start | bytes 1048576 | tf_op jit(solution)/shard_map/all_to_all | solution.py:34
  36.2 3.0 %all-to-all-done = bf16[2,2,65536]{2,1,0:T(2,128)(2,1)S(1)} async-done(((bf16[2,2,65536]{2,1,0:T(2,128)(2,1)}), bf16[2,2,65536]{2,1,0:T(2,128)(2,1)S(1)}, u32[]{:S(2)}, u32[]{:S(2)}) %all-to-all-start) | async-done | bytes 524320 | tf_op jit(solution)/shard_map/all_to_all | solution.py:34
  39.2 6.1 %all-to-all-start.3 = ((bf16[16,2,1,4]{3,1,2,0:T(2,128)(2,1)}), bf16[16,2,1,4]{3,1,2,0:T(2,128)(2,1)S(1)}, u32[]{:S(2)}, u32[]{:S(2)}) async-start(bf16[16,2,1,4]{3,1,2,0:T(2,128)(2,1)} %copy.105), calls=%async_computation.3 | async-start | bytes 16384 | tf_op jit(solution)/shard_map/all_to_all | solution.py:53
  45.4 4.2 %reshape.297 = bf16[1024,2,8,16]{3,2,1,0:T(8,128)(2,1)} reshape(bf16[2,2,65536]{2,1,0:T(2,128)(2,1)S(1)} %all-to-all-done) | data formatting | bytes 1048576
  49.5 4.9 %copy.124 = bf16[8,2,16,2,512]{4,3,2,1,0:T(2,128)(2,1)S(1)} copy(bf16[8,2,16,2,512]{2,0,1,4,3:T(8,128)(2,1)} %bitcast.160) | data formatting | bytes 1048576 | tf_op jit(solution)/shard_map/all_to_all | solution.py:34
  56.0 6.1 %all-to-all-start.1 = ((bf16[16,2,16,512]{3,2,1,0:T(8,128)(2,1)}), bf16[16,2,16,512]{3,2,1,0:T(8,128)(2,1)}, u32[]{:S(2)}, u32[]{:S(2)}) async-start(bf16[16,2,16,512]{3,2,1,0:T(8,128)(2,1)} %broadcast_select_fusion.1), calls=%async_computation.1 | async-start | bytes 1048576 | tf_op jit(solution)/shard_map/all_to_all | solution.py:50
  65.7 10.8 %all-to-all-done.1 = bf16[16,2,16,512]{3,2,1,0:T(8,128)(2,1)} async-done(((bf16[16,2,16,512]{3,2,1,0:T(8,128)(2,1)}), bf16[16,2,16,512]{3,2,1,0:T(8,128)(2,1)}, u32[]{:S(2)}, u32[]{:S(2)}) %all-to-all-start.1) | async-done | bytes 524320 | tf_op jit(solution)/shard_map/all_to_all | solution.py:50
  84.3 141.2 %while.16 = (s32[]{:T(128)}, bf16[16,256,128]{2,1,0:T(8,128)(2,1)}, f32[16,256,128]{2,1,0:T(8,128)S(1)}, f32[16,256,128]{2,1,0:T(8,128)}, bf16[16,256,128]{2,1,0...) while((s32[]{:T(128)}, bf16[16,256,128]{2,1,0:T(8,128)(2,1)}, ...), condition=%wide.region_5.6_spmd.clone, body=%wide.region_1.5_spmd.clone.sunk | while | flops 102038784 | bytes 2638799 | solution.py:119
  105.9 1.7 fusion.97
  141.2 1.7 fusion.97
  150.0 1.7 fusion.97
  167.7 1.7 fusion.97
  176.5 1.7 fusion.97
  185.3 1.7 fusion.97
  203.0 1.7 fusion.97
  225.6 1.9 bitcast_reduce_fusion
  229.1 28.7 %all_to_all.69 = f32[16,2,16,512]{3,2,1,0:T(8,128)S(1)} all-to-all(f32[16,2,16,512]{3,2,1,0:T(8,128)S(1)} %scatter_fusion), channel_id=1, replica_groups=mesh['dp'=16,'mp'=2] {'dp'}, dimensions={0} | all-to-all | bytes 2097152 | tf_op jit(solution)/shard_map/all_to_all | solution.py:139
  260.7 3.6 %all-to-all-start.5 = ((f32[16,2,16,512]{3,2,1,0:T(8,128)}), f32[16,2,16,512]{3,2,1,0:T(8,128)S(1)}, u32[]{:S(2)}, u32[]{:S(2)}) async-start(f32[16,2,16,512]{3,2,1,0:T(8,128)} %copy.119), calls=%async_computation.5 | async-start | bytes 2097152 | tf_op jit(solution)/shard_map/all_to_all | solution.py:144
  265.4 2.3 copy.136
  269.3 9.7 %all-to-all-done.5 = f32[16,2,16,512]{3,2,1,0:T(8,128)S(1)} async-done(((f32[16,2,16,512]{3,2,1,0:T(8,128)}), f32[16,2,16,512]{3,2,1,0:T(8,128)S(1)}, u32[]{:S(2)}, u32[]{:S(2)}) %all-to-all-start.5) | async-done | bytes 1048608 | tf_op jit(solution)/shard_map/all_to_all | solution.py:144
  (205 shorter events, 134.4 us)
Async XLA Ops:
  2.0 25.1 %all-to-all-start.2 = ((bf16[8,2,1,8]{0,1,2,3:T(2,128)(2,1)}), bf16[8,2,1,8]{0,1,2,3:T(2,128)(2,1)S(1)}, u32[]{:S(2)}, u32[]{:S(2)}) async-start(bf16[8,2,1,8]{0,1,2,3:T(2,128)(2,1)} %copy.100), calls=%async_computation.2 | async-start | bytes 8192 | tf_op jit(solution)/shard_map/all_to_all | solution.py:35
  9.2 5.9 %copy-start.4 = (s32[16]{0:T(128)}, s32[16]{0:T(128)S(1)}, u32[]{:S(2)}) copy-start(s32[16]{0:T(128)S(1)} %fusion.46) | copy-start | bytes 196
  9.2 5.8 %copy-start.3 = (bf16[2,1,128,512]{3,2,1,0:T(8,128)(2,1)S(1)}, bf16[2,1,128,512]{3,2,1,0:T(8,128)(2,1)}, u32[]{:S(2)}) copy-start(bf16[2,1,128,512]{3,2,1,0:T(8,128)(2,1)} %param.11) | copy-start | bytes 786436
  9.2 5.9 %copy-start.1 = (bf16[1,128,4096]{2,1,0:T(8,128)(2,1)S(1)}, bf16[1,128,4096]{2,1,0:T(8,128)(2,1)}, u32[]{:S(2)}) copy-start(bf16[1,128,4096]{2,1,0:T(8,128)(2,1)} %param.12) | copy-start | bytes 3145732
  27.1 6.4 %copy-start.2 = (bf16[1,128,4096]{2,1,0:T(8,128)(2,1)S(1)}, bf16[1,128,4096]{2,1,0:T(8,128)(2,1)}, u32[]{:S(2)}) copy-start(bf16[1,128,4096]{2,1,0:T(8,128)(2,1)} %param.10) | copy-start | bytes 3145732
  27.1 12.1 %all-to-all-start = ((bf16[2,2,65536]{2,1,0:T(2,128)(2,1)}), bf16[2,2,65536]{2,1,0:T(2,128)(2,1)S(1)}, u32[]{:S(2)}, u32[]{:S(2)}) async-start(bf16[2,2,65536]{2,1,0:T(2,128)(2,1)} %reshape.296), calls=%async_computation | async-start | bytes 1048576 | tf_op jit(solution)/shard_map/all_to_all | solution.py:34
  39.2 16.8 %all-to-all-start.3 = ((bf16[16,2,1,4]{3,1,2,0:T(2,128)(2,1)}), bf16[16,2,1,4]{3,1,2,0:T(2,128)(2,1)S(1)}, u32[]{:S(2)}, u32[]{:S(2)}) async-start(bf16[16,2,1,4]{3,1,2,0:T(2,128)(2,1)} %copy.105), calls=%async_computation.3 | async-start | bytes 16384 | tf_op jit(solution)/shard_map/all_to_all | solution.py:53
  56.0 20.6 %all-to-all-start.1 = ((bf16[16,2,16,512]{3,2,1,0:T(8,128)(2,1)}), bf16[16,2,16,512]{3,2,1,0:T(8,128)(2,1)}, u32[]{:S(2)}, u32[]{:S(2)}) async-start(bf16[16,2,16,512]{3,2,1,0:T(8,128)(2,1)} %broadcast_select_fusion.1), calls=%async_computation.1 | async-start | bytes 1048576 | tf_op jit(solution)/shard_map/all_to_all | solution.py:50
  65.7 18.6 %copy-start = (f32[16,256,128]{2,1,0:T(8,128)S(1)}, f32[16,256,128]{2,1,0:T(8,128)}, u32[]{:S(2)}) copy-start(f32[16,256,128]{2,1,0:T(8,128)} %custom-call.11) | copy-start | bytes 6291460
  228.3 29.6 %copy-start.5 = (s32[16]{0:T(128)S(1)}, s32[16]{0:T(128)}, u32[]{:S(2)}) copy-start(s32[16]{0:T(128)} %copy-done.4) | copy-start | bytes 196
  260.7 18.4 %all-to-all-start.5 = ((f32[16,2,16,512]{3,2,1,0:T(8,128)}), f32[16,2,16,512]{3,2,1,0:T(8,128)S(1)}, u32[]{:S(2)}, u32[]{:S(2)}) async-start(f32[16,2,16,512]{3,2,1,0:T(8,128)} %copy.119), calls=%async_computation.5 | async-start | bytes 2097152 | tf_op jit(solution)/shard_map/all_to_all | solution.py:144
where the time goes:
time: 284 us; the launch traced here: 280 us
  matrix products  94.2 us (33%)
  local copies, waits for them, and re-layouts  69.5 us (24%)
  blocking collectives  28.7 us (10%)
  loops' own time  27.4 us (10%)
  starting transfers between devices  23.6 us (8%)
  waiting for transfers between devices  23.6 us (8%)
  other arithmetic  11.4 us (4%)
    all_to_all x1, blocking collectives, per_device(): lax.all_to_all(buffer, 'dp', split_axis=0, concat_axis=0, tiled=True)  28.7 us
    another operation x1, loops' own time, per_device(): lax.map(block_step, (query_blocks, grad_blocks, kv_index))  27.4 us
    dot_general x16, matrix products, block_step(): lax.dot_general(weights_b, g_rows, down, preferred_element_type=jnp.float32)  27 us
    dynamic_slice x16, local copies, waits for them, and re-layouts, per_device(): lax.map(block_step, (query_blocks, grad_blocks, kv_index))  19.7 us
    unnamed x21, local copies, waits for them, and re-layouts  19.3 us
    dot_general x16, matrix products, block_step(): attn_out = jnp.dot(weights_b, v_head, preferred_element_type=jnp.float32)  17.7 us
    dot_general x16, matrix products, block_step(): lax.dot_general(g_rows, v_head, across, preferred_element_type=jnp.float32)  16.8 us
    dot_general x16, matrix products, block_step(): lax.dot_general(q_rows, k_head, across, preferred_element_type=jnp.float32)  14.8 us
  transfers between devices with their start and end apart: 5, of which 3 were waited for; matrix products, arithmetic and copies ran while one was open for 16% of the time, Pallas kernels for 0%

commit v1 on v0

v1 whole, which is shorter than its diff:
```python
import functools
import math

import jax
import jax.numpy as jnp
from jax import lax
from jax.experimental import pallas as pl
from jax.experimental.pallas import tpu as pltpu
from jax.sharding import PartitionSpec as P

DH = 128
MESH = pl.DeviceIdType.MESH
BF16 = jnp.bfloat16
F32 = jnp.float32
ACROSS = (((1,), (1,)), ((), ()))


def split_rows(rows):
    size = min(rows, 512)
    while rows % size:
        size //= 2
    return size, rows // size


def over_blocks(rows, body):
    size, count = split_rows(rows)
    if count == 1:
        body(0, size)
    else:

        @pl.loop(0, count)
        def _(b):
            body(pl.multiple_of(b * size, size), size)


def kernel(
    dp,
    mp,
    kv,
    group,
    slot,
    pages_ref,
    scales_ref,
    send_col,
    send_row,
    recv_col,
    recv_row,
    length_ref,
    q_hbm,
    g_hbm,
    rkv_hbm,
    dq_hbm,
    dkv_hbm,
    pool_hbm,
    q_buf,
    g_buf,
    rkv_buf,
    dq_buf,
    dkv_buf,
    pool_buf,
    pick,
    pick_t,
    take,
    take_t,
    slab,
    grouped,
    outgoing,
    arrived,
    back,
    returned,
    summed,
    part_out,
    part_in,
    in_sem,
    out_sem,
    mp_send,
    mp_recv,
    dp_send,
    dp_recv,
    rt_send,
    rt_recv,
    fm_send,
    fm_recv,
):
    my_dp = lax.axis_index("dp")
    my_mp = lax.axis_index("mp")
    store_rows = pages_ref.shape[0]
    resp_len = q_buf.shape[0]
    prompt_len = take.shape[0] // 2
    total = prompt_len + resp_len
    inv_root = 1.0 / DH**0.5
    to_exp2 = inv_root * math.log2(math.e)

    barrier = pltpu.get_barrier_semaphore()

    @pl.loop(1, dp)
    def _(k):
        pl.semaphore_signal(
            barrier, inc=1, device_id={"dp": lax.rem(my_dp + k, dp)}, device_id_type=MESH
        )

    for k in range(1, mp):
        pl.semaphore_signal(
            barrier, inc=1, device_id={"mp": lax.rem(my_mp + k, mp)}, device_id_type=MESH
        )

    loads = [
        pltpu.make_async_copy(rkv_hbm, rkv_buf, in_sem.at[0]),
        pltpu.make_async_copy(q_hbm.at[0], q_buf, in_sem.at[1]),
        pltpu.make_async_copy(g_hbm.at[0], g_buf, in_sem.at[2]),
    ]
    for load in loads:
        load.start()

    for head in range(mp * kv):
        lanes = slice(head * DH, (head + 1) * DH)
        scaled = pages_ref[:, lanes].astype(F32) * scales_ref[:, head : head + 1]
        slab[head] = scaled.astype(BF16)
    pl.semaphore_wait(barrier, dp + mp - 2)

    my_rows = pl.ds(pl.multiple_of(my_mp * store_rows, store_rows), store_rows)
    for j in range(kv):
        for k in range(1, mp):
            other = lax.rem(my_mp + k, mp)
            pltpu.make_async_remote_copy(
                src_ref=slab.at[other * kv + j],
                dst_ref=grouped.at[j, my_rows],
                send_sem=mp_send.at[j],
                recv_sem=mp_recv.at[j],
                device_id={"mp": other},
                device_id_type=MESH,
            ).start()
    for j in range(kv):
        grouped[j, my_rows] = slab[my_mp * kv + j]

    def build(out_ref, codes_ref, by_column):
        def body(start, size):
            shape = (size, out_ref.shape[1])
            if by_column:
                hit = codes_ref[pl.ds(start, size), :] == lax.broadcasted_iota(jnp.int32, shape, 1)
            else:
                hit = codes_ref[...] == lax.broadcasted_iota(jnp.int32, shape, 0) + start
            out_ref[pl.ds(start, size), :] = jnp.where(hit, 1.0, 0.0).astype(BF16)

        over_blocks(out_ref.shape[0], body)

    def select(out_ref, matrix, operand):
        def body(start, size):
            rows = pl.ds(start, size)
            out_ref[rows, :] = jnp.dot(
                matrix[rows, :], operand, preferred_element_type=F32
            ).astype(out_ref.dtype)

        over_blocks(out_ref.shape[0], body)

    build(pick, send_col, True)

    my_slot = pl.ds(pl.multiple_of(my_dp * slot, slot), slot)

    def exchange(j, source, target, send_sem, recv_sem):
        @pl.loop(1, dp)
        def _(k):
            other = lax.rem(my_dp + k, dp)
            pltpu.make_async_remote_copy(
                src_ref=source.at[j, pl.ds(pl.multiple_of(other * slot, slot), slot)],
                dst_ref=target.at[j, my_slot],
                send_sem=send_sem.at[j],
                recv_sem=recv_sem.at[j],
                device_id={"dp": other},
                device_id_type=MESH,
            ).start()

        target[j, my_slot] = source[j, my_slot]

    def wait_bytes(view, sem):
        pltpu.make_async_copy(view, view, sem).wait()

    dp_rows = pl.ds(0, (dp - 1) * slot)
    mp_rows = pl.ds(0, (mp - 1) * store_rows)
    for j in range(kv):
        if mp > 1:
            wait_bytes(grouped.at[j, mp_rows], mp_recv.at[j])
        select(outgoing.at[j], pick, grouped[j])
        exchange(j, outgoing, arrived, dp_send, dp_recv)

    build(take, recv_col, True)
    build(take_t, recv_row, False)
    build(pick_t, send_row, False)
    for load in loads:
        load.wait()

    length = length_ref[0]
    live = lax.broadcasted_iota(jnp.int32, (resp_len, DH), 0) < length
    own_shape = (resp_len, 2 * resp_len)
    causal = lax.broadcasted_iota(jnp.int32, own_shape, 0) <= lax.rem(
        lax.broadcasted_iota(jnp.int32, own_shape, 1), resp_len
    )

    for j in range(kv):
        lanes = slice(j * DH, (j + 1) * DH)
        wait_bytes(arrived.at[j, dp_rows], dp_recv.at[j])
        prompt = jnp.dot(take[...], arrived[j], preferred_element_type=F32).astype(BF16)
        keys = jnp.concatenate([prompt[:prompt_len], rkv_buf[0, 0, :, lanes]], 0)
        values = jnp.concatenate([prompt[prompt_len:], rkv_buf[1, 0, :, lanes]], 0)
        keys_t = keys.astype(F32).T.astype(BF16)
        key_grad = jnp.zeros((total, DH), F32)
        value_grad = jnp.zeros((total, DH), F32)
        for first in range(0, group, 2):
            base = (j * group + first) * DH
            heads = [slice(base, base + DH), slice(base + DH, base + 2 * DH)]
            queries = jnp.concatenate([q_buf[:, h] for h in heads], 0)
            grads = jnp.concatenate(
                [jnp.where(live, g_buf[:, h], jnp.zeros((), BF16)) for h in heads], 0
            )
            scores = lax.dot_general(keys, queries, ACROSS, preferred_element_type=F32)
            scores = jnp.concatenate(
                [scores[:prompt_len], jnp.where(causal, scores[prompt_len:], -1e30)], 0
            )
            top = jnp.max(scores, axis=0, keepdims=True)
            powers = jnp.exp2((scores - top) * to_exp2)
            weights = powers * (1.0 / jnp.sum(powers, axis=0, keepdims=True))
            weights_b = weights.astype(BF16)
            grad_weights = lax.dot_general(values, grads, ACROSS, preferred_element_type=F32)
            delta = jnp.sum(weights_b.astype(F32) * grad_weights, axis=0, keepdims=True)
            grad_scores = (weights * (grad_weights - delta)).astype(BF16)
            query_t = jnp.dot(keys_t, grad_scores, preferred_element_type=F32) * inv_root
            query_grad = query_t.T.astype(BF16)
            for i, h in enumerate(heads):
                dq_buf[:, h] = query_grad[i * resp_len : (i + 1) * resp_len]
            key_grad += jnp.dot(grad_scores, queries, preferred_element_type=F32)
            value_grad += jnp.dot(weights_b, grads, preferred_element_type=F32)
        key_grad = key_grad * inv_root
        dkv_buf[0, 0, :, lanes] = key_grad[prompt_len:].astype(BF16)
        dkv_buf[1, 0, :, lanes] = value_grad[prompt_len:].astype(BF16)
        prompt_grad = jnp.concatenate([key_grad[:prompt_len], value_grad[:prompt_len]], 0)
        select(back.at[j], take_t, prompt_grad.astype(BF16))
        exchange(j, back, returned, rt_send, rt_recv)

    stores = [
        pltpu.make_async_copy(dq_buf, dq_hbm.at[0], out_sem.at[0]),
        pltpu.make_async_copy(dkv_buf, dkv_hbm, out_sem.at[1]),
    ]
    for store in stores:
        store.start()

    def column(m, j):
        return pl.ds(pl.multiple_of((m * kv + j) * DH, DH), DH)

    for j in range(kv):
        wait_bytes(returned.at[j, dp_rows], rt_recv.at[j])
        select(summed, pick_t, returned[j])
        for k in range(1, mp):
            other = lax.rem(my_mp + k, mp)
            rows = pl.ds(pl.multiple_of(other * store_rows, store_rows), store_rows)
            part_out[other * kv + j] = summed[rows, :].astype(BF16)
            pltpu.make_async_remote_copy(
                src_ref=part_out.at[other * kv + j],
                dst_ref=part_in.at[j, my_mp],
                send_sem=fm_send.at[j],
                recv_sem=fm_recv.at[j],
                device_id={"mp": other},
                device_id_type=MESH,
            ).start()
        pool_buf[:, column(my_mp, j)] = summed[my_rows, :]
    for j in range(kv):
        if mp > 1:
            wait_bytes(part_in.at[j, pl.ds(0, mp - 1)], fm_recv.at[j])
        for k in range(1, mp):
            other = lax.rem(my_mp + k, mp)
            pool_buf[:, column(other, j)] = part_in[j, other].astype(F32)
    last = pltpu.make_async_copy(pool_buf, pool_hbm, out_sem.at[2])
    last.start()
    for j in range(kv):
        if mp > 1:
            wait_bytes(grouped.at[j, mp_rows], mp_send.at[j])
            wait_bytes(part_in.at[j, pl.ds(0, mp - 1)], fm_send.at[j])
        wait_bytes(arrived.at[j, dp_rows], dp_send.at[j])
        wait_bytes(returned.at[j, dp_rows], rt_send.at[j])
    for store in stores:
        store.wait()
    last.wait()


def per_device(resp_q, resp_kv, d_out, lengths, fork, page_table, pool_pages, pool_scales):
    dp = lax.axis_size("dp")
    mp = lax.axis_size("mp")
    my_dp = lax.axis_index("dp")
    pool_dev, _, page_rows, width = pool_pages.shape
    heads_kv = pool_scales.shape[-1]
    kv = heads_kv // mp
    pages_prompt = page_table.shape[1]
    prompt_len = pages_prompt * page_rows
    resp_len = resp_q.shape[1]
    group = resp_q.shape[2] // DH // kv
    group_pages = mp * pool_dev
    slot = 2 * page_rows
    store_rows = pool_dev * slot
    group_rows = mp * store_rows
    slots = dp * slot

    wanted = jnp.take(page_table, fork, axis=0)
    here = wanted // group_pages == my_dp
    rows = jnp.sum(jnp.where(here, wanted % group_pages + 1, 0), axis=1) - 1
    inside = jnp.arange(slot, dtype=jnp.int32)
    send_code = jnp.where(rows[:, None] >= 0, rows[:, None] * slot + inside[None, :], -1)
    sources = jnp.take(wanted, my_dp, axis=0) // group_pages
    recv_code = sources[None, :, None] * slot + inside.reshape(2, 1, page_rows)
    scales = jnp.broadcast_to(
        pool_scales.astype(F32)[:, :, None, :], (pool_dev, 2, page_rows, heads_kv)
    )

    vmem = pl.BlockSpec(memory_space=pltpu.VMEM)
    smem = pl.BlockSpec(memory_space=pltpu.SMEM)
    hbm = pl.BlockSpec(memory_space=pl.ANY)
    dma = pltpu.SemaphoreType.DMA
    total = prompt_len + resp_len
    d_query, d_kv, d_pool = pl.pallas_call(
        functools.partial(kernel, dp, mp, kv, group, slot),
        out_shape=(
            jax.ShapeDtypeStruct(resp_q.shape, BF16),
            jax.ShapeDtypeStruct(resp_kv.shape, BF16),
            jax.ShapeDtypeStruct((store_rows, width), F32),
        ),
        in_specs=[vmem] * 6 + [smem] + [hbm] * 3,
        out_specs=(hbm, hbm, hbm),
        scratch_shapes=[
            pltpu.VMEM(resp_q.shape[1:], BF16),
            pltpu.VMEM(d_out.shape[1:], BF16),
            pltpu.VMEM(resp_kv.shape, BF16),
            pltpu.VMEM(resp_q.shape[1:], BF16),
            pltpu.VMEM(resp_kv.shape, BF16),
            pltpu.VMEM((store_rows, width), F32),
            pltpu.VMEM((slots, group_rows), BF16),
            pltpu.VMEM((group_rows, slots), BF16),
            pltpu.VMEM((2 * prompt_len, slots), BF16),
            pltpu.VMEM((slots, 2 * prompt_len), BF16),
            pltpu.VMEM((heads_kv, store_rows, DH), BF16),
            pltpu.VMEM((kv, group_rows, DH), BF16),
            pltpu.VMEM((kv, slots, DH), BF16),
            pltpu.VMEM((kv, slots, DH), BF16),
            pltpu.VMEM((kv, slots, DH), BF16),
            pltpu.VMEM((kv, slots, DH), BF16),
            pltpu.VMEM((group_rows, DH), F32),
            pltpu.VMEM((heads_kv, store_rows, DH), BF16),
            pltpu.VMEM((kv, mp, store_rows, DH), BF16),
            dma((3,)),
            dma((3,)),
        ]
        + [dma((kv,))] * 8,
        compiler_params=pltpu.CompilerParams(
            collective_id=0, has_side_effects=True, vmem_limit_bytes=56 * 1024 * 1024
        ),
        cost_estimate=pl.CostEstimate(
            flops=10 * group * kv * resp_len * total * DH,
            bytes_accessed=8 * resp_q.shape[1] * resp_q.shape[2],
            transcendentals=group * kv * resp_len * total,
        ),
    )(
        pool_pages.reshape(store_rows, width),
        scales.reshape(store_rows, heads_kv),
        send_code.reshape(slots, 1),
        send_code.reshape(1, slots),
        recv_code.reshape(2 * prompt_len, 1),
        recv_code.reshape(1, 2 * prompt_len),
        lengths,
        resp_q,
        d_out,
        resp_kv,
    )
    return (d_query, d_kv, d_pool.reshape(pool_pages.shape))


def solution(mesh):
    return jax.shard_map(
        per_device,
        mesh=mesh,
        in_specs=(
            P("dp", None, "mp"),
            P(None, "dp", None, "mp"),
            P("dp", None, "mp"),
            P("dp"),
            P(),
            P(),
            P(("dp", "mp"), None, None, None),
            P(("dp", "mp"), None, None),
        ),
        out_specs=(
            P("dp", None, "mp"),
            P(None, "dp", None, "mp"),
            P(("dp", "mp"), None, None, None),
        ),
        check_vma=False,
    )
```

time: 284 us -> 52.5 us (0.18); the launches traced: 280 us -> 52.3 us
  matrix products: 94.2 us -> 0 us
  local copies, waits for them, and re-layouts: 69.5 us -> 9.72 us
  Pallas kernels: 0 us -> 40.8 us
  blocking collectives: 28.7 us -> 0 us
  loops' own time: 27.4 us -> 0 us
  starting transfers between devices: 23.6 us -> 0 us
  waiting for transfers between devices: 23.6 us -> 0 us
  other arithmetic: 11.4 us -> 0.39 us
    dot_general x97 -> x0, matrix products: 94.2 us -> none  [the longest x16 27 us: block_step(): lax.dot_general(weights_b, g_rows, down, preferred_element_type=jnp.float32)]
    pallas_call x0 -> x1, Pallas kernels: none -> 40.8 us  [per_device(): pl.pallas_call(functools.partial(kernel, dp, mp, kv, group, slot), out_sh...]
    all_to_all x1 -> x0, blocking collectives: 28.7 us -> none  [per_device(): lax.all_to_all(buffer, 'dp', split_axis=0, concat_axis=0, tiled=True)]
    another operation x1 -> x0, loops' own time: 27.4 us -> none  [per_device(): lax.map(block_step, (query_blocks, grad_blocks, kv_index))]
    all_to_all x5 -> x0, starting transfers between devices: 23.6 us -> none  [the longest x1 6.14 us: per_device(): lax.all_to_all(jnp.take(regscales, send_rows, axis=0), 'dp', split_axis=0...]
    all_to_all x5 -> x0, waiting for transfers between devices: 23.6 us -> none  [the longest x1 10.8 us: per_device(): lax.all_to_all(jnp.take(regrouped, send_rows, axis=0), 'dp', split_axis=0...]
    dynamic_slice x16 -> x0, local copies, waits for them, and re-layouts: 19.7 us -> none  [per_device(): lax.map(block_step, (query_blocks, grad_blocks, kv_index))]
    unnamed x21 -> x14, local copies, waits for them, and re-layouts: 19.3 us -> 5.45 us
  transfers between devices with their start and end apart: 5 -> 0, of which waited for: 3 -> 0; matrix products, arithmetic and copies ran while one was open for 16% -> 0% of each run, Pallas kernels for 0% -> 0%
where the time goes in v1:
time: 52.5 us; the launch traced here: 52.3 us
  Pallas kernels  40.8 us (78%)
  local copies, waits for them, and re-layouts  9.72 us (19%)
  between operations  1.37 us (3%)
    pallas_call x1, Pallas kernels, per_device(): pl.pallas_call(functools.partial(kernel, dp, mp, kv, group, slot), out_sh...  40.8 us
    unnamed x14, local copies, waits for them, and re-layouts  5.45 us
    select_n x2, local copies, waits for them, and re-layouts, per_device(): jnp.where(rows[:, None] >= 0, rows[:, None] * slot + inside[None, :], -1)  1.64 us
    add x2, local copies, waits for them, and re-layouts, per_device(): recv_code = sources[None, :, None] * slot + inside.reshape(2, 1, page_rows)  1.41 us

profile of v1, /device:TPU:0, one launch (start us, length us, event | category | flops | bytes accessed | tf_op | source)
XLA Modules:
  0.0 52.3 jit_solution(7824418272911298060)
XLA Ops:
  1.3 0.0 copy-start.4
  1.3 0.6 %copy-done.4 = s32[16]{0:T(128)S(1)} copy-done((s32[16]{0:T(128)S(1)}, s32[16]{0:T(128)}, u32[]{:S(2)}) %copy-start.4) | copy-done | bytes 88
  1.9 0.0 copy-start.2
  2.0 0.6 %copy-done.2 = s32[32,8]{0,1:T(8,128)S(1)} copy-done((s32[32,8]{0,1:T(8,128)S(1)}, s32[32,8]{0,1:T(8,128)}, u32[]{:S(2)}) %copy-start.2) | copy-done | bytes 1048
  2.6 0.1 copy.12
  2.7 0.6 %gather_fusion = s32[16,8]{1,0:T(8,128)S(1)} fusion(s32[32,8]{1,0:T(8,128)S(1)} %copy.12, s32[1024]{0:T(1024)S(1)} %pad_clamp_fusion), kind=kCustom, calls=%fused_computation | custom fusion | bytes 1088 | tf_op jit(solution)/shard_map/jit(_take)/gather | solution.py:301
  3.3 0.2 fusion.3
  3.5 0.1 broadcast_add_fusion
  3.6 0.7 %add.114.recv_row = s32[1,256]{1,0:T(1,128)} reshape(s32[2,8,16]{2,1,0:T(8,128)S(1)} %broadcast_add_fusion) | data formatting | bytes 2048 | tf_op jit(solution)/shard_map/add | solution.py:307
  4.2 0.1 add_select_fusion.2
  4.3 0.7 %select_n.77.send_row = s32[1,512]{1,0:T(1,128)} reshape(s32[16,32]{1,0:T(8,128)S(1)} %add_select_fusion.2) | data formatting | bytes 4096 | tf_op jit(solution)/shard_map/jit(_where)/select_n | solution.py:305
  5.0 0.0 copy-start.3
  5.0 0.8 %add.117.recv_col = s32[256,1]{1,0:T(8,128)} reshape(s32[2,8,16]{2,1,0:T(8,128)S(1)} %broadcast_add_fusion) | data formatting | bytes 2048 | tf_op jit(solution)/shard_map/add | solution.py:307
  5.7 0.0 copy-done.3
  5.7 0.7 %broadcast_in_dim.44 = f32[8,2,16,8]{3,2,1,0:T(8,128)} broadcast(bf16[8,2,8]{2,1,0:T(2,128)(2,1)S(1)} %copy-done.3), dimensions={0,1,3} | broadcast | bytes 8448 | tf_op jit(solution)/shard_map/broadcast_in_dim | solution.py:308
  6.4 1.0 %select_n.82.send_col = s32[512,1]{1,0:T(8,128)} reshape(s32[16,32]{1,0:T(8,128)S(1)} %add_select_fusion.2) | data formatting | bytes 4096 | tf_op jit(solution)/shard_map/jit(_where)/select_n | solution.py:305
  7.4 40.8 %shard_map.103 = (bf16[1,128,4096]{2,1,0:T(8,128)(2,1)}, bf16[2,1,128,512]{3,2,1,0:T(8,128)(2,1)}, f32[256,1024]{1,0:T(8,128)}) custom-call(bf16[256,1024]{1,0:T(8,128)(2,1)} %bitcast.11, f32[256,8]{1,0:T(8,128)} %bitcast.10, s32[512,1]{1,0:T(8,128)} %select_n.82.send_col, s32[1,512]{1,0:T(1,128)} %select_n.77.send_row, s32[256,1]{1,0:T(8,128)} %add.117.recv_col, ...), custom_call_target="tpu_custom_call" | custom-call | flops 1342177280 | bytes 4194304 | tf_op jit(solution)/shard_map/pallas_call | solution.py:317
  48.2 0.0 copy-start.1
  48.2 0.0 copy-start
  48.2 2.4 %copy.19 = bf16[1,128,4096]{2,1,0:T(8,128)(2,1)} copy(bf16[1,128,4096]{2,1,0:T(8,128)(2,1)} %get-tuple-element.25) | data formatting | bytes 2097152
  50.6 0.0 copy-done.1
  50.6 0.7 %copy.20 = bf16[2,1,128,512]{3,2,1,0:T(8,128)(2,1)} copy(bf16[2,1,128,512]{3,2,1,0:T(8,128)(2,1)S(1)} %copy-done.1) | data formatting | bytes 524288
  51.3 0.0 copy-done
  51.3 1.0 %copy.21 = f32[8,2,16,1024]{3,2,1,0:T(8,128)} copy(f32[8,2,16,1024]{3,2,1,0:T(8,128)S(1)} %bitcast.9) | data formatting | bytes 2097152
  (7 shorter events, 0.1 us)
Async XLA Ops:
  1.3 0.7 %copy-start.4 = (s32[16]{0:T(128)S(1)}, s32[16]{0:T(128)}, u32[]{:S(2)}) copy-start(s32[16]{0:T(128)} %param.12) | copy-start | bytes 196
  1.9 0.7 %copy-start.2 = (s32[32,8]{0,1:T(8,128)S(1)}, s32[32,8]{0,1:T(8,128)}, u32[]{:S(2)}) copy-start(s32[32,8]{0,1:T(8,128)} %param.13) | copy-start | bytes 3076
  5.0 0.8 %copy-start.3 = (bf16[8,2,8]{2,1,0:T(2,128)(2,1)S(1)}, bf16[8,2,8]{2,1,0:T(2,128)(2,1)}, u32[]{:S(2)}) copy-start(bf16[8,2,8]{2,1,0:T(2,128)(2,1)} %param.15) | copy-start | bytes 772
  48.2 2.4 %copy-start.1 = (bf16[2,1,128,512]{3,2,1,0:T(8,128)(2,1)S(1)}, bf16[2,1,128,512]{3,2,1,0:T(8,128)(2,1)}, u32[]{:S(2)}) copy-start(bf16[2,1,128,512]{3,2,1,0:T(8,128)(2,1)} %get-tuple-element.26) | copy-start | bytes 786436
  48.2 3.1 %copy-start = (f32[256,1024]{1,0:T(8,128)S(1)}, f32[256,1024]{1,0:T(8,128)}, u32[]{:S(2)}) copy-start(f32[256,1024]{1,0:T(8,128)} %get-tuple-element.8) | copy-start | bytes 3145732

commit v2 on v1

v2 whole, which is shorter than its diff:
```python
import functools
import math

import jax
import jax.numpy as jnp
from jax import lax
from jax.experimental import pallas as pl
from jax.experimental.pallas import tpu as pltpu
from jax.sharding import PartitionSpec as P

DH = 128
WIDTH = 1
MESH = pl.DeviceIdType.MESH
BF16 = jnp.bfloat16
F32 = jnp.float32
ACROSS = (((1,), (1,)), ((), ()))


def split_rows(rows):
    size = min(rows, 512)
    while rows % size:
        size //= 2
    return size, rows // size


def over_blocks(rows, body):
    size, count = split_rows(rows)
    if count == 1:
        body(0, size)
    else:

        @pl.loop(0, count)
        def _(b):
            body(pl.multiple_of(b * size, size), size)


def partner_order(count):
    half, quarter = count // 2, count // 4
    order = []
    for i in range(quarter):
        order += [half + i, half + quarter + i, quarter + i]
    rest = [k for k in range(1, count) if k not in order]
    return [k for k in order if 0 < k < count] + rest


def ones_where(hit):
    return jnp.where(hit, 1.0, 0.0).astype(BF16)


def kernel(
    dp,
    mp,
    kv,
    group,
    width,
    scales_ref,
    fork_ref,
    table_ref,
    length_ref,
    pages_hbm,
    q_hbm,
    g_hbm,
    rkv_hbm,
    dq_hbm,
    dkv_hbm,
    pool_hbm,
    pages_ref,
    q_buf,
    g_buf,
    rkv_buf,
    dq_buf,
    dkv_buf,
    pool_buf,
    pick,
    pick_t,
    take,
    take_t,
    slab,
    grouped,
    outgoing,
    arrived,
    back,
    returned,
    summed,
    part_out,
    part_in,
    codes,
    in_sem,
    out_sem,
    mp_send,
    mp_recv,
    dp_send,
    dp_recv,
    rt_send,
    rt_recv,
    fm_send,
    fm_recv,
):
    my_dp = lax.axis_index("dp")
    my_mp = lax.axis_index("mp")
    pool_dev = scales_ref.shape[0]
    store_rows = pages_ref.shape[0]
    slot = store_rows // pool_dev
    page_rows = slot // 2
    group_pages = mp * pool_dev
    pages_prompt = table_ref.shape[0]
    resp_len = q_buf.shape[0]
    prompt_len = pages_prompt * page_rows
    total = prompt_len + resp_len
    chunks = kv // width
    span = width * DH
    inv_root = 1.0 / DH**0.5
    to_exp2 = inv_root * math.log2(math.e)

    pages_load = pltpu.make_async_copy(pages_hbm, pages_ref, in_sem.at[3])
    pages_load.start()
    barrier = pltpu.get_barrier_semaphore()

    @pl.loop(1, dp)
    def _(k):
        pl.semaphore_signal(
            barrier, inc=1, device_id={"dp": lax.rem(my_dp + k, dp)}, device_id_type=MESH
        )

    for k in range(1, mp):
        pl.semaphore_signal(
            barrier, inc=1, device_id={"mp": lax.rem(my_mp + k, mp)}, device_id_type=MESH
        )

    loads = [
        pltpu.make_async_copy(rkv_hbm, rkv_buf, in_sem.at[0]),
        pltpu.make_async_copy(q_hbm.at[0], q_buf, in_sem.at[1]),
        pltpu.make_async_copy(g_hbm.at[0], g_buf, in_sem.at[2]),
    ]
    for load in loads:
        load.start()

    factors = []
    for n in range(pool_dev):
        pair = scales_ref[n].astype(F32)
        for c in range(2):
            factors.append(jnp.broadcast_to(pair[c : c + 1, :], (page_rows, mp * kv)))
    factors = jnp.concatenate(factors, 0)
    pages_load.wait()
    for head in range(mp * kv):
        lanes = slice(head * DH, (head + 1) * DH)
        inner = slice(head % width * DH, (head % width + 1) * DH)
        scaled = pages_ref[:, lanes].astype(F32) * factors[:, head : head + 1]
        slab[head // width, :, inner] = scaled.astype(BF16)
    pl.semaphore_wait(barrier, dp + mp - 2)

    my_rows = pl.ds(pl.multiple_of(my_mp * store_rows, store_rows), store_rows)
    for c in range(chunks):
        for k in range(1, mp):
            other = lax.rem(my_mp + k, mp)
            pltpu.make_async_remote_copy(
                src_ref=slab.at[other * chunks + c],
                dst_ref=grouped.at[c, my_rows],
                send_sem=mp_send.at[c],
                recv_sem=mp_recv.at[c],
                device_id={"mp": other},
                device_id_type=MESH,
            ).start()
    for c in range(chunks):
        grouped[c, my_rows] = slab[my_mp * chunks + c]

    iota = functools.partial(lax.broadcasted_iota, jnp.int32)
    ahead = iota((slot, pick.shape[1]), 1) - iota((slot, pick.shape[1]), 0)

    @pl.loop(0, dp, unroll=4 if dp % 4 == 0 else 1)
    def _(r):
        prompt_id = fork_ref[r]
        code = jnp.int32(-(1 << 20))
        for i in range(pages_prompt):
            page = table_ref[i, prompt_id]
            code = jnp.where(
                lax.div(page, group_pages) == my_dp, lax.rem(page, group_pages) * slot, code
            )
        codes[r] = code
        pick[pl.ds(pl.multiple_of(r * slot, slot), slot), :] = ones_where(ahead == code)

    def select(out_ref, matrix, operand):
        def body(start, size):
            rows = pl.ds(start, size)
            out_ref[rows, :] = jnp.dot(
                matrix[rows, :], operand, preferred_element_type=F32
            ).astype(out_ref.dtype)

        over_blocks(out_ref.shape[0], body)

    my_slot = pl.ds(pl.multiple_of(my_dp * slot, slot), slot)

    def exchange(c, source, target, send_sem, recv_sem):
        for k in partner_order(dp):
            other = lax.rem(my_dp + k, dp)
            pltpu.make_async_remote_copy(
                src_ref=source.at[c, pl.ds(pl.multiple_of(other * slot, slot), slot)],
                dst_ref=target.at[c, my_slot],
                send_sem=send_sem.at[c],
                recv_sem=recv_sem.at[c],
                device_id={"dp": other},
                device_id_type=MESH,
            ).start()
        target[c, my_slot] = source[c, my_slot]

    def wait_bytes(view, sem):
        pltpu.make_async_copy(view, view, sem).wait()

    dp_rows = pl.ds(0, (dp - 1) * slot)
    mp_rows = pl.ds(0, (mp - 1) * store_rows)
    for c in range(chunks):
        if mp > 1:
            wait_bytes(grouped.at[c, mp_rows], mp_recv.at[c])
        select(outgoing.at[c], pick, grouped[c])
        exchange(c, outgoing, arrived, dp_send, dp_recv)

    my_prompt = fork_ref[my_dp]
    sources = [
        lax.div(table_ref[i, my_prompt], group_pages) * slot for i in range(pages_prompt)
    ]
    ahead = iota((page_rows, dp * slot), 1) - iota((page_rows, dp * slot), 0)
    for c in range(2):
        for i in range(pages_prompt):
            take[pl.ds(c * prompt_len + i * page_rows, page_rows), :] = ones_where(
                ahead == sources[i] + c * page_rows
            )

    lane = iota((1, DH), 1)

    def transposed(out_ref, block, starts, piece):
        wanted = jnp.zeros((1, DH), jnp.int32)
        for i, start in enumerate(starts):
            wanted = jnp.where(lax.div(lane, piece) == i, start, wanted)
        wanted = wanted + lax.rem(lane, piece)

        def body(start, size):
            down = iota((size, DH), 0) + start
            out_ref[pl.ds(start, size), block * DH : (block + 1) * DH] = ones_where(down == wanted)

        over_blocks(out_ref.shape[0], body)

    per_block = DH // page_rows
    for block in range(2 * prompt_len // DH):
        pieces = [divmod(block * per_block + i, pages_prompt) for i in range(per_block)]
        starts = [sources[i] + c * page_rows for c, i in pieces]
        transposed(take_t, block, starts, page_rows)
    per_block = DH // slot
    for block in range(dp * slot // DH):
        starts = [codes[block * per_block + i] for i in range(per_block)]
        transposed(pick_t, block, starts, slot)
    for load in loads:
        load.wait()

    length = length_ref[0]
    live = lax.broadcasted_iota(jnp.int32, (resp_len, DH), 0) < length
    own_shape = (resp_len, 2 * resp_len)
    causal = lax.broadcasted_iota(jnp.int32, own_shape, 0) <= lax.rem(
        lax.broadcasted_iota(jnp.int32, own_shape, 1), resp_len
    )

    def attend(j, prompt):
        lanes = slice(j * DH, (j + 1) * DH)
        keys = jnp.concatenate([prompt[:prompt_len], rkv_buf[0, 0, :, lanes]], 0)
        values = jnp.concatenate([prompt[prompt_len:], rkv_buf[1, 0, :, lanes]], 0)
        keys_t = keys.astype(F32).T.astype(BF16)
        key_grad = jnp.zeros((total, DH), F32)
        value_grad = jnp.zeros((total, DH), F32)
        for first in range(0, group, 2):
            base = (j * group + first) * DH
            heads = [slice(base, base + DH), slice(base + DH, base + 2 * DH)]
            queries = jnp.concatenate([q_buf[:, h] for h in heads], 0)
            grads = jnp.concatenate(
                [jnp.where(live, g_buf[:, h], jnp.zeros((), BF16)) for h in heads], 0
            )
            scores = lax.dot_general(keys, queries, ACROSS, preferred_element_type=F32)
            scores = jnp.concatenate(
                [scores[:prompt_len], jnp.where(causal, scores[prompt_len:], -1e30)], 0
            )
            top = jnp.max(scores, axis=0, keepdims=True)
            powers = jnp.exp2((scores - top) * to_exp2)
            weights = powers * (1.0 / jnp.sum(powers, axis=0, keepdims=True))
            weights_b = weights.astype(BF16)
            grad_weights = lax.dot_general(values, grads, ACROSS, preferred_element_type=F32)
            delta = jnp.sum(weights_b.astype(F32) * grad_weights, axis=0, keepdims=True)
            grad_scores = (weights * (grad_weights - delta)).astype(BF16)
            query_t = jnp.dot(keys_t, grad_scores, preferred_element_type=F32) * inv_root
            query_grad = query_t.T.astype(BF16)
            for i, h in enumerate(heads):
                dq_buf[:, h] = query_grad[i * resp_len : (i + 1) * resp_len]
            key_grad += jnp.dot(grad_scores, queries, preferred_element_type=F32)
            value_grad += jnp.dot(weights_b, grads, preferred_element_type=F32)
        key_grad = key_grad * inv_root
        dkv_buf[0, 0, :, lanes] = key_grad[prompt_len:].astype(BF16)
        dkv_buf[1, 0, :, lanes] = value_grad[prompt_len:].astype(BF16)
        prompt_grad = jnp.concatenate([key_grad[:prompt_len], value_grad[:prompt_len]], 0)
        return prompt_grad.astype(BF16)

    for c in range(chunks):
        wait_bytes(arrived.at[c, dp_rows], dp_recv.at[c])
        prompt = jnp.dot(take[...], arrived[c], preferred_element_type=F32).astype(BF16)
        parts = [
            attend(c * width + i, prompt[:, i * DH : (i + 1) * DH]) for i in range(width)
        ]
        prompt_grad = jnp.concatenate(parts, 1) if width > 1 else parts[0]
        select(back.at[c], take_t, prompt_grad)
        exchange(c, back, returned, rt_send, rt_recv)

    stores = [
        pltpu.make_async_copy(dq_buf, dq_hbm.at[0], out_sem.at[0]),
        pltpu.make_async_copy(dkv_buf, dkv_hbm, out_sem.at[1]),
    ]
    for store in stores:
        store.start()

    def column(m, c):
        return pl.ds(pl.multiple_of((m * chunks + c) * span, span), span)

    for c in range(chunks):
        wait_bytes(returned.at[c, dp_rows], rt_recv.at[c])
        select(summed, pick_t, returned[c])
        for k in range(1, mp):
            other = lax.rem(my_mp + k, mp)
            rows = pl.ds(pl.multiple_of(other * store_rows, store_rows), store_rows)
            part_out[other * chunks + c] = summed[rows, :].astype(BF16)
            pltpu.make_async_remote_copy(
                src_ref=part_out.at[other * chunks + c],
                dst_ref=part_in.at[c, my_mp],
                send_sem=fm_send.at[c],
                recv_sem=fm_recv.at[c],
                device_id={"mp": other},
                device_id_type=MESH,
            ).start()
        pool_buf[:, column(my_mp, c)] = summed[my_rows, :]
    for c in range(chunks):
        if mp > 1:
            wait_bytes(part_in.at[c, pl.ds(0, mp - 1)], fm_recv.at[c])
        for k in range(1, mp):
            other = lax.rem(my_mp + k, mp)
            pool_buf[:, column(other, c)] = part_in[c, other].astype(F32)
    last = pltpu.make_async_copy(pool_buf, pool_hbm, out_sem.at[2])
    last.start()
    for c in range(chunks):
        if mp > 1:
            wait_bytes(grouped.at[c, mp_rows], mp_send.at[c])
            wait_bytes(part_in.at[c, pl.ds(0, mp - 1)], fm_send.at[c])
        wait_bytes(arrived.at[c, dp_rows], dp_send.at[c])
        wait_bytes(returned.at[c, dp_rows], rt_send.at[c])
    for store in stores:
        store.wait()
    last.wait()


def settle(dq_in, dkv_in, pool_in, dq_out, dkv_out, pool_out, sem):
    copies = []

    def piece(source, target):
        copies.append(pltpu.make_async_copy(source, target, sem.at[len(copies)]))

    rows = dq_in.shape[1] // 4
    for i in range(4):
        piece(dq_in.at[:, pl.ds(i * rows, rows)], dq_out.at[:, pl.ds(i * rows, rows)])
    rows = pool_in.shape[0] // 4
    for i in range(4):
        piece(pool_in.at[pl.ds(i * rows, rows)], pool_out.at[pl.ds(i * rows, rows)])
    piece(dkv_in, dkv_out)
    for copy in copies:
        copy.start()
    for copy in copies:
        copy.wait()


def per_device(resp_q, resp_kv, d_out, lengths, fork, page_table, pool_pages, pool_scales):
    dp = lax.axis_size("dp")
    mp = lax.axis_size("mp")
    pool_dev, _, page_rows, pool_width = pool_pages.shape
    heads_kv = pool_scales.shape[-1]
    kv = heads_kv // mp
    width = WIDTH if kv % WIDTH == 0 else 1
    chunks, span = kv // width, width * DH
    pages_prompt = page_table.shape[1]
    prompt_len = pages_prompt * page_rows
    resp_len = resp_q.shape[1]
    group = resp_q.shape[2] // DH // kv
    slot = 2 * page_rows
    store_rows = pool_dev * slot
    group_rows = mp * store_rows
    slots = dp * slot

    vmem = pl.BlockSpec(memory_space=pltpu.VMEM)
    smem = pl.BlockSpec(memory_space=pltpu.SMEM)
    hbm = pl.BlockSpec(memory_space=pl.ANY)
    dma = pltpu.SemaphoreType.DMA
    total = prompt_len + resp_len
    out_shape = (
        jax.ShapeDtypeStruct(resp_q.shape, BF16),
        jax.ShapeDtypeStruct(resp_kv.shape, BF16),
        jax.ShapeDtypeStruct((store_rows, pool_width), F32),
    )
    buffers = [
        ((store_rows, pool_width), BF16),
        (resp_q.shape[1:], BF16),
        (d_out.shape[1:], BF16),
        (resp_kv.shape, BF16),
        (resp_q.shape[1:], BF16),
        (resp_kv.shape, BF16),
        ((store_rows, pool_width), F32),
        ((slots, group_rows), BF16),
        ((group_rows, slots), BF16),
        ((2 * prompt_len, slots), BF16),
        ((slots, 2 * prompt_len), BF16),
        ((mp * chunks, store_rows, span), BF16),
        ((chunks, group_rows, span), BF16),
        ((chunks, slots, span), BF16),
        ((chunks, slots, span), BF16),
        ((chunks, slots, span), BF16),
        ((chunks, slots, span), BF16),
        ((group_rows, span), F32),
        ((mp * chunks, store_rows, span), BF16),
        ((chunks, mp, store_rows, span), BF16),
    ]
    results = pl.pallas_call(
        functools.partial(kernel, dp, mp, kv, group, width),
        out_shape=out_shape,
        in_specs=[vmem] + [smem] * 3 + [pl.BlockSpec(memory_space=pltpu.HBM)] * 4,
        out_specs=(hbm, hbm, hbm),
        scratch_shapes=[pltpu.VMEM(shape, kind) for shape, kind in buffers]
        + [pltpu.SMEM((dp,), jnp.int32), dma((4,)), dma((3,))]
        + [dma((chunks,))] * 8,
        compiler_params=pltpu.CompilerParams(
            collective_id=0,
            has_side_effects=True,
            vmem_limit_bytes=56 << 20,
        ),
        cost_estimate=pl.CostEstimate(
            flops=10 * group * kv * resp_len * total * DH,
            bytes_accessed=8 * resp_q.shape[1] * resp_q.shape[2],
            transcendentals=group * kv * resp_len * total,
        ),
    )(
        pool_scales,
        fork,
        page_table.T,
        lengths,
        pool_pages.reshape(store_rows, pool_width),
        resp_q,
        d_out,
        resp_kv,
    )
    d_query, d_kv, d_pool = pl.pallas_call(
        settle,
        out_shape=out_shape,
        in_specs=[hbm] * 3,
        out_specs=(hbm, hbm, hbm),
        scratch_shapes=[dma((9,))],
    )(*results)
    return (d_query, d_kv, d_pool.reshape(pool_pages.shape))


def solution(mesh):
    return jax.shard_map(
        per_device,
        mesh=mesh,
        in_specs=(
            P("dp", None, "mp"),
            P(None, "dp", None, "mp"),
            P("dp", None, "mp"),
            P("dp"),
            P(),
            P(),
            P(("dp", "mp"), None, None, None),
            P(("dp", "mp"), None, None),
        ),
        out_specs=(
            P("dp", None, "mp"),
            P(None, "dp", None, "mp"),
            P(("dp", "mp"), None, None, None),
        ),
        check_vma=False,
    )
```

time: 52.5 us -> 114 us (2.17)
  Pallas kernels: 40.8 us -> 112 us
  local copies, waits for them, and re-layouts: 9.72 us -> 0 us
    pallas_call x1 -> x2, Pallas kernels: 40.8 us -> 112 us  [the longest x1 72.7 us: per_device(): pl.pallas_call(settle, out_shape=out_shape, in_specs=[hbm] * 3, out_specs...]
    unnamed x14 -> x0, local copies, waits for them, and re-layouts: 5.45 us -> none
    select_n x2 -> x0, local copies, waits for them, and re-layouts: 1.64 us -> none  [per_device(): jnp.where(rows[:, None] >= 0, rows[:, None] * slot + inside[None, :], -1)]
    add x2 -> x0, local copies, waits for them, and re-layouts: 1.41 us -> none  [per_device(): recv_code = sources[None, :, None] * slot + inside.reshape(2, 1, page_rows)]
where the time goes in v2:
time: 114 us
  Pallas kernels  112 us (98%)
  between operations  1.29 us (1%)
    pallas_call x1, Pallas kernels, per_device(): pl.pallas_call(settle, out_shape=out_shape, in_specs=[hbm] * 3, out_specs...  72.7 us
    pallas_call x1, Pallas kernels, per_device(): pl.pallas_call(functools.partial(kernel, dp, mp, kv, group, width), out_s...  39.7 us

profile of v2, /device:TPU:0, one launch (start us, length us, event | category | flops | bytes accessed | tf_op | source)
XLA Modules:
  0.0 113.7 jit_solution(11107346576599239077)
XLA Ops:
  1.3 39.7 %shard_map.103 = (bf16[1,128,4096]{2,1,0:T(8,128)(2,1)}, bf16[2,1,128,512]{3,2,1,0:T(8,128)(2,1)}, f32[256,1024]{1,0:T(8,128)}) custom-call(bf16[8,2,8]{2,1,0:T(2,128)(2,1)} %scales_ref.1, s32[16]{0:T(128)} %fork_ref.1, s32[8,32]{1,0:T(8,128)} %bitcast.5, s32[1]{0:T(128)S(6)} %copy.11.length_ref, bf16[256,1024]{1,0:T(8,128)(2,1)} %bitcast.4, ...), custom_call_target="tpu_custom_call" | custom-call | flops 1342177280 | bytes 4194304 | tf_op jit(solution)/shard_map/pallas_call | solution.py:421
  41.0 72.7 %shard_map.104 = (bf16[1,128,4096]{2,1,0:T(8,128)(2,1)}, bf16[2,1,128,512]{3,2,1,0:T(8,128)(2,1)}, f32[256,1024]{1,0:T(8,128)}) custom-call(bf16[1,128,4096]{2,1,0:T(8,128)(2,1)} %get-tuple-element.9.dq_in, bf16[2,1,128,512]{3,2,1,0:T(8,128)(2,1)} %get-tuple-element.10.dkv_in, f32[256,1024]{1,0:T(8,128)} %get-tuple-element.11.pool_in), custom_call_target="tpu_custom_call" | custom-call | tf_op jit(solution)/shard_map/pallas_call | solution.py:449

commit v3 on v2

--- a/solution.py
+++ b/solution.py
@@ -9,7 +9,7 @@
 from jax.sharding import PartitionSpec as P
 
 DH = 128
-WIDTH = 1
+WIDTH = 2
 MESH = pl.DeviceIdType.MESH
 BF16 = jnp.bfloat16
 F32 = jnp.float32
@@ -350,23 +350,28 @@
     last.wait()
 
 
-def settle(dq_in, dkv_in, pool_in, dq_out, dkv_out, pool_out, sem):
-    copies = []
-
-    def piece(source, target):
-        copies.append(pltpu.make_async_copy(source, target, sem.at[len(copies)]))
-
+def settle(dq_in, dkv_in, pool_in, dq_out, dkv_out, pool_out, dq_buf, dkv_buf, pool_buf, sem):
+    pieces = []
     rows = dq_in.shape[1] // 4
     for i in range(4):
-        piece(dq_in.at[:, pl.ds(i * rows, rows)], dq_out.at[:, pl.ds(i * rows, rows)])
+        at = (slice(None), pl.ds(i * rows, rows))
+        pieces.append((dq_in.at[at], dq_buf.at[at], dq_out.at[at]))
     rows = pool_in.shape[0] // 4
     for i in range(4):
-        piece(pool_in.at[pl.ds(i * rows, rows)], pool_out.at[pl.ds(i * rows, rows)])
-    piece(dkv_in, dkv_out)
-    for copy in copies:
-        copy.start()
-    for copy in copies:
-        copy.wait()
+        at = pl.ds(i * rows, rows)
+        pieces.append((pool_in.at[at], pool_buf.at[at], pool_out.at[at]))
+    pieces.append((dkv_in, dkv_buf, dkv_out))
+    reads, writes = [], []
+    for i, (source, middle, target) in enumerate(pieces):
+        reads.append(pltpu.make_async_copy(source, middle, sem.at[0, i]))
+        writes.append(pltpu.make_async_copy(middle, target, sem.at[1, i]))
+    for read in reads:
+        read.start()
+    for read, write in zip(reads, writes):
+        read.wait()
+        write.start()
+    for write in writes:
+        write.wait()
 
 
 def per_device(resp_q, resp_kv, d_out, lengths, fork, page_table, pool_pages, pool_scales):
@@ -451,7 +456,8 @@
         out_shape=out_shape,
         in_specs=[hbm] * 3,
         out_specs=(hbm, hbm, hbm),
-        scratch_shapes=[dma((9,))],
+        scratch_shapes=[pltpu.VMEM(o.shape, o.dtype) for o in out_shape] + [dma((2, 9))],
+        compiler_params=pltpu.CompilerParams(vmem_limit_bytes=56 << 20),
     )(*results)
     return (d_query, d_kv, d_pool.reshape(pool_pages.shape))
 

time: 114 us -> 50.1 us (0.44)
  Pallas kernels: 112 us -> 48.6 us
    pallas_call x1, Pallas kernels: 72.7 us -> 2.5 us  [per_device(): pl.pallas_call(settle, out_shape=out_shape, in_specs=[hbm] * 3, out_specs...]
    pallas_call x1, Pallas kernels: 39.7 us -> 46.1 us  [per_device(): pl.pallas_call(functools.partial(kernel, dp, mp, kv, group, width), out_s...]
where the time goes in v3:
time: 50.1 us; the launch traced here: 49.9 us
  Pallas kernels  48.6 us (97%)
  between operations  1.29 us (3%)
    pallas_call x1, Pallas kernels, per_device(): pl.pallas_call(functools.partial(kernel, dp, mp, kv, group, width), out_s...  46.1 us
    pallas_call x1, Pallas kernels, per_device(): pl.pallas_call(settle, out_shape=out_shape, in_specs=[hbm] * 3, out_specs...  2.5 us

profile of v3, /device:TPU:0, one launch (start us, length us, event | category | flops | bytes accessed | tf_op | source)
XLA Modules:
  0.0 49.9 jit_solution(91690265130462569)
XLA Ops:
  1.3 46.1 %shard_map.103 = (bf16[1,128,4096]{2,1,0:T(8,128)(2,1)}, bf16[2,1,128,512]{3,2,1,0:T(8,128)(2,1)}, f32[256,1024]{1,0:T(8,128)}) custom-call(bf16[8,2,8]{2,1,0:T(2,128)(2,1)} %scales_ref.1, s32[16]{0:T(128)} %fork_ref.1, s32[8,32]{1,0:T(8,128)} %bitcast.5, s32[1]{0:T(128)S(6)} %copy.11.length_ref, bf16[256,1024]{1,0:T(8,128)(2,1)} %bitcast.4, ...), custom_call_target="tpu_custom_call" | custom-call | flops 1342177280 | bytes 4194304 | tf_op jit(solution)/shard_map/pallas_call | solution.py:426
  47.4 2.5 %shard_map.104 = (bf16[1,128,4096]{2,1,0:T(8,128)(2,1)}, bf16[2,1,128,512]{3,2,1,0:T(8,128)(2,1)}, f32[256,1024]{1,0:T(8,128)}) custom-call(bf16[1,128,4096]{2,1,0:T(8,128)(2,1)} %get-tuple-element.9.dq_in, bf16[2,1,128,512]{3,2,1,0:T(8,128)(2,1)} %get-tuple-element.10.dkv_in, f32[256,1024]{1,0:T(8,128)} %get-tuple-element.11.pool_in), custom_call_target="tpu_custom_call" | custom-call | tf_op jit(solution)/shard_map/pallas_call | solution.py:454

commit v4 on v3

--- a/solution.py
+++ b/solution.py
@@ -9,7 +9,7 @@
 from jax.sharding import PartitionSpec as P
 
 DH = 128
-WIDTH = 2
+WIDTH = 1
 MESH = pl.DeviceIdType.MESH
 BF16 = jnp.bfloat16
 F32 = jnp.float32
@@ -84,6 +84,12 @@
     summed,
     part_out,
     part_in,
+    queries,
+    grads,
+    scores,
+    grad_weights,
+    weights_b,
+    grad_scores,
     codes,
     in_sem,
     out_sem,
@@ -251,45 +257,50 @@
     for load in loads:
         load.wait()
 
-    length = length_ref[0]
-    live = lax.broadcasted_iota(jnp.int32, (resp_len, DH), 0) < length
-    own_shape = (resp_len, 2 * resp_len)
-    causal = lax.broadcasted_iota(jnp.int32, own_shape, 0) <= lax.rem(
-        lax.broadcasted_iota(jnp.int32, own_shape, 1), resp_len
-    )
+    live = iota((resp_len, DH), 0) < length_ref[0]
+    for h in range(kv * group):
+        lanes = slice(h * DH, (h + 1) * DH)
+        rows = pl.ds(h % group * resp_len, resp_len)
+        queries[h // group, rows, :] = q_buf[:, lanes]
+        grads[h // group, rows, :] = jnp.where(live, g_buf[:, lanes], jnp.zeros((), BF16))
+    causal = iota((resp_len, resp_len), 0) <= iota((resp_len, resp_len), 1)
 
     def attend(j, prompt):
         lanes = slice(j * DH, (j + 1) * DH)
         keys = jnp.concatenate([prompt[:prompt_len], rkv_buf[0, 0, :, lanes]], 0)
         values = jnp.concatenate([prompt[prompt_len:], rkv_buf[1, 0, :, lanes]], 0)
         keys_t = keys.astype(F32).T.astype(BF16)
-        key_grad = jnp.zeros((total, DH), F32)
-        value_grad = jnp.zeros((total, DH), F32)
-        for first in range(0, group, 2):
-            base = (j * group + first) * DH
-            heads = [slice(base, base + DH), slice(base + DH, base + 2 * DH)]
-            queries = jnp.concatenate([q_buf[:, h] for h in heads], 0)
-            grads = jnp.concatenate(
-                [jnp.where(live, g_buf[:, h], jnp.zeros((), BF16)) for h in heads], 0
+        scores[...] = lax.dot_general(keys, queries[j], ACROSS, preferred_element_type=F32)
+        grad_weights[...] = lax.dot_general(
+            values, grads[j], ACROSS, preferred_element_type=F32
+        )
+        for i in range(group):
+            across = slice(i * resp_len, (i + 1) * resp_len)
+            block = jnp.concatenate(
+                [
+                    scores[:prompt_len, across],
+                    jnp.where(causal, scores[prompt_len:, across], -1e30),
+                ],
+                0,
             )
-            scores = lax.dot_general(keys, queries, ACROSS, preferred_element_type=F32)
-            scores = jnp.concatenate(
-                [scores[:prompt_len], jnp.where(causal, scores[prompt_len:], -1e30)], 0
-            )
-            top = jnp.max(scores, axis=0, keepdims=True)
-            powers = jnp.exp2((scores - top) * to_exp2)
+            top = jnp.max(block, axis=0, keepdims=True)
+            powers = jnp.exp2((block - top) * to_exp2)
             weights = powers * (1.0 / jnp.sum(powers, axis=0, keepdims=True))
-            weights_b = weights.astype(BF16)
-            grad_weights = lax.dot_general(values, grads, ACROSS, preferred_element_type=F32)
-            delta = jnp.sum(weights_b.astype(F32) * grad_weights, axis=0, keepdims=True)
-            grad_scores = (weights * (grad_weights - delta)).astype(BF16)
-            query_t = jnp.dot(keys_t, grad_scores, preferred_element_type=F32) * inv_root
-            query_grad = query_t.T.astype(BF16)
-            for i, h in enumerate(heads):
-                dq_buf[:, h] = query_grad[i * resp_len : (i + 1) * resp_len]
-            key_grad += jnp.dot(grad_scores, queries, preferred_element_type=F32)
-            value_grad += jnp.dot(weights_b, grads, preferred_element_type=F32)
-        key_grad = key_grad * inv_root
+            rounded = weights.astype(BF16)
+            change = grad_weights[:, across]
+            delta = jnp.sum(rounded.astype(F32) * change, axis=0, keepdims=True)
+            weights_b[:, across] = rounded
+            grad_scores[:, across] = (weights * (change - delta)).astype(BF16)
+        query_t = jnp.dot(keys_t, grad_scores[...], preferred_element_type=F32) * inv_root
+        for i in range(group):
+            h = j * group + i
+            dq_buf[:, h * DH : (h + 1) * DH] = query_t[
+                :, i * resp_len : (i + 1) * resp_len
+            ].T.astype(BF16)
+        key_grad = (
+            jnp.dot(grad_scores[...], queries[j], preferred_element_type=F32) * inv_root
+        )
+        value_grad = jnp.dot(weights_b[...], grads[j], preferred_element_type=F32)
         dkv_buf[0, 0, :, lanes] = key_grad[prompt_len:].astype(BF16)
         dkv_buf[1, 0, :, lanes] = value_grad[prompt_len:].astype(BF16)
         prompt_grad = jnp.concatenate([key_grad[:prompt_len], value_grad[:prompt_len]], 0)
@@ -422,6 +433,12 @@
         ((group_rows, span), F32),
         ((mp * chunks, store_rows, span), BF16),
         ((chunks, mp, store_rows, span), BF16),
+        ((kv, group * resp_len, DH), BF16),
+        ((kv, group * resp_len, DH), BF16),
+        ((total, group * resp_len), F32),
+        ((total, group * resp_len), F32),
+        ((total, group * resp_len), BF16),
+        ((total, group * resp_len), BF16),
     ]
     results = pl.pallas_call(
         functools.partial(kernel, dp, mp, kv, group, width),

time: 50.1 us -> 43.3 us (0.86)
  Pallas kernels: 48.6 us -> 41.8 us
    pallas_call x1, Pallas kernels: 46.1 us -> 39.3 us  [per_device(): pl.pallas_call(functools.partial(kernel, dp, mp, kv, group, width), out_s...]
where the time goes in v4:
time: 43.3 us; the launch traced here: 43 us
  Pallas kernels  41.8 us (97%)
  between operations  1.29 us (3%)
    pallas_call x1, Pallas kernels, per_device(): pl.pallas_call(functools.partial(kernel, dp, mp, kv, group, width), out_s...  39.3 us
    pallas_call x1, Pallas kernels, per_device(): pl.pallas_call(settle, out_shape=out_shape, in_specs=[hbm] * 3, out_specs...  2.5 us

profile of v4, /device:TPU:0, one launch (start us, length us, event | category | flops | bytes accessed | tf_op | source)
XLA Modules:
  0.0 43.0 jit_solution(9087218513354381413)
XLA Ops:
  1.3 39.3 %shard_map.103 = (bf16[1,128,4096]{2,1,0:T(8,128)(2,1)}, bf16[2,1,128,512]{3,2,1,0:T(8,128)(2,1)}, f32[256,1024]{1,0:T(8,128)}) custom-call(bf16[8,2,8]{2,1,0:T(2,128)(2,1)} %scales_ref.1, s32[16]{0:T(128)} %fork_ref.1, s32[8,32]{1,0:T(8,128)} %bitcast.5, s32[1]{0:T(128)S(6)} %copy.11.length_ref, bf16[256,1024]{1,0:T(8,128)(2,1)} %bitcast.4, ...), custom_call_target="tpu_custom_call" | custom-call | flops 1342177280 | bytes 4194304 | tf_op jit(solution)/shard_map/pallas_call | solution.py:443
  40.5 2.5 %shard_map.104 = (bf16[1,128,4096]{2,1,0:T(8,128)(2,1)}, bf16[2,1,128,512]{3,2,1,0:T(8,128)(2,1)}, f32[256,1024]{1,0:T(8,128)}) custom-call(bf16[1,128,4096]{2,1,0:T(8,128)(2,1)} %get-tuple-element.9.dq_in, bf16[2,1,128,512]{3,2,1,0:T(8,128)(2,1)} %get-tuple-element.10.dkv_in, f32[256,1024]{1,0:T(8,128)} %get-tuple-element.11.pool_in), custom_call_target="tpu_custom_call" | custom-call | tf_op jit(solution)/shard_map/pallas_call | solution.py:471

commit v5 on v4

--- a/solution.py
+++ b/solution.py
@@ -9,7 +9,6 @@
 from jax.sharding import PartitionSpec as P
 
 DH = 128
-WIDTH = 1
 MESH = pl.DeviceIdType.MESH
 BF16 = jnp.bfloat16
 F32 = jnp.float32
@@ -52,7 +51,6 @@
     mp,
     kv,
     group,
-    width,
     scales_ref,
     fork_ref,
     table_ref,
@@ -105,16 +103,14 @@
     my_dp = lax.axis_index("dp")
     my_mp = lax.axis_index("mp")
     pool_dev = scales_ref.shape[0]
-    store_rows = pages_ref.shape[0]
-    slot = store_rows // pool_dev
-    page_rows = slot // 2
+    page_rows = pages_ref.shape[2]
+    store_rows = pool_dev * page_rows
     group_pages = mp * pool_dev
     pages_prompt = table_ref.shape[0]
     resp_len = q_buf.shape[0]
     prompt_len = pages_prompt * page_rows
     total = prompt_len + resp_len
-    chunks = kv // width
-    span = width * DH
+    chunks = 2 * kv
     inv_root = 1.0 / DH**0.5
     to_exp2 = inv_root * math.log2(math.e)
 
@@ -146,13 +142,13 @@
         pair = scales_ref[n].astype(F32)
         for c in range(2):
             factors.append(jnp.broadcast_to(pair[c : c + 1, :], (page_rows, mp * kv)))
-    factors = jnp.concatenate(factors, 0)
     pages_load.wait()
-    for head in range(mp * kv):
-        lanes = slice(head * DH, (head + 1) * DH)
-        inner = slice(head % width * DH, (head % width + 1) * DH)
-        scaled = pages_ref[:, lanes].astype(F32) * factors[:, head : head + 1]
-        slab[head // width, :, inner] = scaled.astype(BF16)
+    for c in range(2):
+        column = jnp.concatenate(factors[c::2], 0)
+        for head in range(mp * kv):
+            stored = pages_ref[:, c, :, head * DH : (head + 1) * DH].reshape(store_rows, DH)
+            scaled = stored.astype(F32) * column[:, head : head + 1]
+            slab[head * 2 + c] = scaled.astype(BF16)
     pl.semaphore_wait(barrier, dp + mp - 2)
 
     my_rows = pl.ds(pl.multiple_of(my_mp * store_rows, store_rows), store_rows)
@@ -171,7 +167,7 @@
         grouped[c, my_rows] = slab[my_mp * chunks + c]
 
     iota = functools.partial(lax.broadcasted_iota, jnp.int32)
-    ahead = iota((slot, pick.shape[1]), 1) - iota((slot, pick.shape[1]), 0)
+    ahead = iota((page_rows, pick.shape[1]), 1) - iota((page_rows, pick.shape[1]), 0)
 
     @pl.loop(0, dp, unroll=4 if dp % 4 == 0 else 1)
     def _(r):
@@ -180,10 +176,10 @@
         for i in range(pages_prompt):
             page = table_ref[i, prompt_id]
             code = jnp.where(
-                lax.div(page, group_pages) == my_dp, lax.rem(page, group_pages) * slot, code
+                lax.div(page, group_pages) == my_dp, lax.rem(page, group_pages) * page_rows, code
             )
         codes[r] = code
-        pick[pl.ds(pl.multiple_of(r * slot, slot), slot), :] = ones_where(ahead == code)
+        pick[pl.ds(pl.multiple_of(r * page_rows, page_rows), page_rows), :] = ones_where(ahead == code)
 
     def select(out_ref, matrix, operand):
         def body(start, size):
@@ -194,13 +190,13 @@
 
         over_blocks(out_ref.shape[0], body)
 
-    my_slot = pl.ds(pl.multiple_of(my_dp * slot, slot), slot)
+    my_slot = pl.ds(pl.multiple_of(my_dp * page_rows, page_rows), page_rows)
 
     def exchange(c, source, target, send_sem, recv_sem):
         for k in partner_order(dp):
             other = lax.rem(my_dp + k, dp)
             pltpu.make_async_remote_copy(
-                src_ref=source.at[c, pl.ds(pl.multiple_of(other * slot, slot), slot)],
+                src_ref=source.at[c, pl.ds(pl.multiple_of(other * page_rows, page_rows), page_rows)],
                 dst_ref=target.at[c, my_slot],
                 send_sem=send_sem.at[c],
                 recv_sem=recv_sem.at[c],
@@ -212,7 +208,7 @@
     def wait_bytes(view, sem):
         pltpu.make_async_copy(view, view, sem).wait()
 
-    dp_rows = pl.ds(0, (dp - 1) * slot)
+    dp_rows = pl.ds(0, (dp - 1) * page_rows)
     mp_rows = pl.ds(0, (mp - 1) * store_rows)
     for c in range(chunks):
         if mp > 1:
@@ -222,38 +218,33 @@
 
     my_prompt = fork_ref[my_dp]
     sources = [
-        lax.div(table_ref[i, my_prompt], group_pages) * slot for i in range(pages_prompt)
+        lax.div(table_ref[i, my_prompt], group_pages) * page_rows for i in range(pages_prompt)
     ]
-    ahead = iota((page_rows, dp * slot), 1) - iota((page_rows, dp * slot), 0)
-    for c in range(2):
-        for i in range(pages_prompt):
-            take[pl.ds(c * prompt_len + i * page_rows, page_rows), :] = ones_where(
-                ahead == sources[i] + c * page_rows
-            )
+    ahead = iota((page_rows, dp * page_rows), 1) - iota((page_rows, dp * page_rows), 0)
+    for i in range(pages_prompt):
+        take[pl.ds(i * page_rows, page_rows), :] = ones_where(ahead == sources[i])
 
     lane = iota((1, DH), 1)
 
-    def transposed(out_ref, block, starts, piece):
-        wanted = jnp.zeros((1, DH), jnp.int32)
-        for i, start in enumerate(starts):
-            wanted = jnp.where(lax.div(lane, piece) == i, start, wanted)
-        wanted = wanted + lax.rem(lane, piece)
-
-        def body(start, size):
-            down = iota((size, DH), 0) + start
-            out_ref[pl.ds(start, size), block * DH : (block + 1) * DH] = ones_where(down == wanted)
-
-        over_blocks(out_ref.shape[0], body)
-
-    per_block = DH // page_rows
-    for block in range(2 * prompt_len // DH):
-        pieces = [divmod(block * per_block + i, pages_prompt) for i in range(per_block)]
-        starts = [sources[i] + c * page_rows for c, i in pieces]
-        transposed(take_t, block, starts, page_rows)
-    per_block = DH // slot
-    for block in range(dp * slot // DH):
-        starts = [codes[block * per_block + i] for i in range(per_block)]
-        transposed(pick_t, block, starts, slot)
+    def transposed(out_ref, starts):
+        per_block = DH // page_rows
+        for block in range(-(-len(starts) // per_block)):
+            wanted = jnp.zeros((1, DH), jnp.int32)
+            for i, start in enumerate(starts[block * per_block : (block + 1) * per_block]):
+                wanted = jnp.where(lax.div(lane, page_rows) == i, start, wanted)
+            wanted = wanted + lax.rem(lane, page_rows)
+            columns = min(DH, len(starts) * page_rows - block * DH)
+
+            def body(first, size):
+                down = iota((size, DH), 0) + first
+                out_ref[pl.ds(first, size), block * DH : block * DH + columns] = ones_where(
+                    down == wanted
+                )[:, :columns]
+
+            over_blocks(out_ref.shape[0], body)
+
+    transposed(take_t, sources)
+    transposed(pick_t, [codes[r] for r in range(dp)])
     for load in loads:
         load.wait()
 
@@ -265,10 +256,10 @@
         grads[h // group, rows, :] = jnp.where(live, g_buf[:, lanes], jnp.zeros((), BF16))
     causal = iota((resp_len, resp_len), 0) <= iota((resp_len, resp_len), 1)
 
-    def attend(j, prompt):
+    def attend(j, prompt_keys, prompt_values):
         lanes = slice(j * DH, (j + 1) * DH)
-        keys = jnp.concatenate([prompt[:prompt_len], rkv_buf[0, 0, :, lanes]], 0)
-        values = jnp.concatenate([prompt[prompt_len:], rkv_buf[1, 0, :, lanes]], 0)
+        keys = jnp.concatenate([prompt_keys, rkv_buf[0, 0, :, lanes]], 0)
+        values = jnp.concatenate([prompt_values, rkv_buf[1, 0, :, lanes]], 0)
         keys_t = keys.astype(F32).T.astype(BF16)
         scores[...] = lax.dot_general(keys, queries[j], ACROSS, preferred_element_type=F32)
         grad_weights[...] = lax.dot_general(
@@ -297,24 +288,25 @@
             dq_buf[:, h * DH : (h + 1) * DH] = query_t[
                 :, i * resp_len : (i + 1) * resp_len
             ].T.astype(BF16)
+        value_grad = jnp.dot(weights_b[...], grads[j], preferred_element_type=F32)
+        give_back(2 * j + 1, value_grad)
         key_grad = (
             jnp.dot(grad_scores[...], queries[j], preferred_element_type=F32) * inv_root
         )
-        value_grad = jnp.dot(weights_b[...], grads[j], preferred_element_type=F32)
+        give_back(2 * j, key_grad)
         dkv_buf[0, 0, :, lanes] = key_grad[prompt_len:].astype(BF16)
         dkv_buf[1, 0, :, lanes] = value_grad[prompt_len:].astype(BF16)
-        prompt_grad = jnp.concatenate([key_grad[:prompt_len], value_grad[:prompt_len]], 0)
-        return prompt_grad.astype(BF16)
-
-    for c in range(chunks):
-        wait_bytes(arrived.at[c, dp_rows], dp_recv.at[c])
-        prompt = jnp.dot(take[...], arrived[c], preferred_element_type=F32).astype(BF16)
-        parts = [
-            attend(c * width + i, prompt[:, i * DH : (i + 1) * DH]) for i in range(width)
-        ]
-        prompt_grad = jnp.concatenate(parts, 1) if width > 1 else parts[0]
-        select(back.at[c], take_t, prompt_grad)
-        exchange(c, back, returned, rt_send, rt_recv)
+
+    def give_back(q, grad):
+        select(back.at[q], take_t, grad[:prompt_len].astype(BF16))
+        exchange(q, back, returned, rt_send, rt_recv)
+
+    def prompt_part(q):
+        wait_bytes(arrived.at[q, dp_rows], dp_recv.at[q])
+        return jnp.dot(take[...], arrived[q], preferred_element_type=F32).astype(BF16)
+
+    for j in range(kv):
+        attend(j, prompt_part(2 * j), prompt_part(2 * j + 1))
 
     stores = [
         pltpu.make_async_copy(dq_buf, dq_hbm.at[0], out_sem.at[0]),
@@ -323,39 +315,46 @@
     for store in stores:
         store.start()
 
-    def column(m, c):
-        return pl.ds(pl.multiple_of((m * chunks + c) * span, span), span)
-
-    for c in range(chunks):
-        wait_bytes(returned.at[c, dp_rows], rt_recv.at[c])
-        select(summed, pick_t, returned[c])
+    def settled(m, q, block):
+        head = m * kv + q // 2
+        at = (slice(None), q % 2, slice(None), pl.ds(pl.multiple_of(head * DH, DH), DH))
+        pool_buf[at] = block.reshape(pool_dev, page_rows, DH)
+        pltpu.make_async_copy(pool_buf.at[at], pool_hbm.at[at], out_sem.at[2]).start()
+
+    def finish(q):
+        if mp > 1:
+            wait_bytes(part_in.at[q, pl.ds(0, mp - 1)], fm_recv.at[q])
+        for k in range(1, mp):
+            other = lax.rem(my_mp + k, mp)
+            settled(other, q, part_in[q, other].astype(F32))
+
+    order = [2 * j + c for j in range(kv) for c in (1, 0)]
+    for i, q in enumerate(order):
+        wait_bytes(returned.at[q, dp_rows], rt_recv.at[q])
+        select(summed, pick_t, returned[q])
         for k in range(1, mp):
             other = lax.rem(my_mp + k, mp)
             rows = pl.ds(pl.multiple_of(other * store_rows, store_rows), store_rows)
-            part_out[other * chunks + c] = summed[rows, :].astype(BF16)
+            part_out[other * chunks + q] = summed[rows, :].astype(BF16)
             pltpu.make_async_remote_copy(
-                src_ref=part_out.at[other * chunks + c],
-                dst_ref=part_in.at[c, my_mp],
-                send_sem=fm_send.at[c],
-                recv_sem=fm_recv.at[c],
+                src_ref=part_out.at[other * chunks + q],
+                dst_ref=part_in.at[q, my_mp],
+                send_sem=fm_send.at[q],
+                recv_sem=fm_recv.at[q],
                 device_id={"mp": other},
                 device_id_type=MESH,
             ).start()
-        pool_buf[:, column(my_mp, c)] = summed[my_rows, :]
-    for c in range(chunks):
+        settled(my_mp, q, summed[my_rows, :])
+        if i > 0:
+            finish(order[i - 1])
+    finish(order[-1])
+    for q in range(chunks):
         if mp > 1:
-            wait_bytes(part_in.at[c, pl.ds(0, mp - 1)], fm_recv.at[c])
-        for k in range(1, mp):
-            other = lax.rem(my_mp + k, mp)
-            pool_buf[:, column(other, c)] = part_in[c, other].astype(F32)
+            wait_bytes(grouped.at[q, mp_rows], mp_send.at[q])
+            wait_bytes(part_in.at[q, pl.ds(0, mp - 1)], fm_send.at[q])
+        wait_bytes(arrived.at[q, dp_rows], dp_send.at[q])
+        wait_bytes(returned.at[q, dp_rows], rt_send.at[q])
     last = pltpu.make_async_copy(pool_buf, pool_hbm, out_sem.at[2])
-    last.start()
-    for c in range(chunks):
-        if mp > 1:
-            wait_bytes(grouped.at[c, mp_rows], mp_send.at[c])
-            wait_bytes(part_in.at[c, pl.ds(0, mp - 1)], fm_send.at[c])
-        wait_bytes(arrived.at[c, dp_rows], dp_send.at[c])
-        wait_bytes(returned.at[c, dp_rows], rt_send.at[c])
     for store in stores:
         store.wait()
     last.wait()
@@ -388,19 +387,17 @@
 def per_device(resp_q, resp_kv, d_out, lengths, fork, page_table, pool_pages, pool_scales):
     dp = lax.axis_size("dp")
     mp = lax.axis_size("mp")
-    pool_dev, _, page_rows, pool_width = pool_pages.shape
+    pool_dev, _, page_rows, _ = pool_pages.shape
     heads_kv = pool_scales.shape[-1]
     kv = heads_kv // mp
-    width = WIDTH if kv % WIDTH == 0 else 1
-    chunks, span = kv // width, width * DH
+    chunks = 2 * kv
     pages_prompt = page_table.shape[1]
     prompt_len = pages_prompt * page_rows
     resp_len = resp_q.shape[1]
     group = resp_q.shape[2] // DH // kv
-    slot = 2 * page_rows
-    store_rows = pool_dev * slot
+    store_rows = pool_dev * page_rows
     group_rows = mp * store_rows
-    slots = dp * slot
+    slots = dp * page_rows
 
     vmem = pl.BlockSpec(memory_space=pltpu.VMEM)
     smem = pl.BlockSpec(memory_space=pltpu.SMEM)
@@ -410,29 +407,29 @@
     out_shape = (
         jax.ShapeDtypeStruct(resp_q.shape, BF16),
         jax.ShapeDtypeStruct(resp_kv.shape, BF16),
-        jax.ShapeDtypeStruct((store_rows, pool_width), F32),
+        jax.ShapeDtypeStruct(pool_pages.shape, F32),
     )
     buffers = [
-        ((store_rows, pool_width), BF16),
+        (pool_pages.shape, BF16),
         (resp_q.shape[1:], BF16),
         (d_out.shape[1:], BF16),
         (resp_kv.shape, BF16),
         (resp_q.shape[1:], BF16),
         (resp_kv.shape, BF16),
-        ((store_rows, pool_width), F32),
+        (pool_pages.shape, F32),
         ((slots, group_rows), BF16),
         ((group_rows, slots), BF16),
-        ((2 * prompt_len, slots), BF16),
-        ((slots, 2 * prompt_len), BF16),
-        ((mp * chunks, store_rows, span), BF16),
-        ((chunks, group_rows, span), BF16),
-        ((chunks, slots, span), BF16),
-        ((chunks, slots, span), BF16),
-        ((chunks, slots, span), BF16),
-        ((chunks, slots, span), BF16),
-        ((group_rows, span), F32),
-        ((mp * chunks, store_rows, span), BF16),
-        ((chunks, mp, store_rows, span), BF16),
+        ((prompt_len, slots), BF16),
+        ((slots, prompt_len), BF16),
+        ((mp * chunks, store_rows, DH), BF16),
+        ((chunks, group_rows, DH), BF16),
+        ((chunks, slots, DH), BF16),
+        ((chunks, slots, DH), BF16),
+        ((chunks, slots, DH), BF16),
+        ((chunks, slots, DH), BF16),
+        ((group_rows, DH), F32),
+        ((mp * chunks, store_rows, DH), BF16),
+        ((chunks, mp, store_rows, DH), BF16),
         ((kv, group * resp_len, DH), BF16),
         ((kv, group * resp_len, DH), BF16),
         ((total, group * resp_len), F32),
@@ -441,7 +438,7 @@
         ((total, group * resp_len), BF16),
     ]
     results = pl.pallas_call(
-        functools.partial(kernel, dp, mp, kv, group, width),
+        functools.partial(kernel, dp, mp, kv, group),
         out_shape=out_shape,
         in_specs=[vmem] + [smem] * 3 + [pl.BlockSpec(memory_space=pltpu.HBM)] * 4,
         out_specs=(hbm, hbm, hbm),
@@ -463,7 +460,7 @@
         fork,
         page_table.T,
         lengths,
-        pool_pages.reshape(store_rows, pool_width),
+        pool_pages,
         resp_q,
         d_out,
         resp_kv,
@@ -476,7 +473,7 @@
         scratch_shapes=[pltpu.VMEM(o.shape, o.dtype) for o in out_shape] + [dma((2, 9))],
         compiler_params=pltpu.CompilerParams(vmem_limit_bytes=56 << 20),
     )(*results)
-    return (d_query, d_kv, d_pool.reshape(pool_pages.shape))
+    return (d_query, d_kv, d_pool)
 
 
 def solution(mesh):

time: 43.3 us -> 45.9 us (1.060); the launches traced: 43 us -> 45.1 us
  Pallas kernels: 41.8 us -> 43.8 us
    pallas_call x1, Pallas kernels: 39.3 us -> 41.3 us  [per_device(): pl.pallas_call(functools.partial(kernel, dp, mp, kv, group), out_shape=ou...]
where the time goes in v5:
time: 45.9 us; the launch traced here: 45.1 us
  Pallas kernels  43.8 us (95%)
  between operations  1.29 us (3%)
    pallas_call x1, Pallas kernels, per_device(): pl.pallas_call(functools.partial(kernel, dp, mp, kv, group), out_shape=ou...  41.3 us
    pallas_call x1, Pallas kernels, per_device(): pl.pallas_call(settle, out_shape=out_shape, in_specs=[hbm] * 3, out_specs...  2.5 us

profile of v5, /device:TPU:0, one launch (start us, length us, event | category | flops | bytes accessed | tf_op | source)
XLA Modules:
  0.0 45.1 jit_solution(2405492129631050526)
XLA Ops:
  1.3 41.3 %shard_map.103 = (bf16[1,128,4096]{2,1,0:T(8,128)(2,1)}, bf16[2,1,128,512]{3,2,1,0:T(8,128)(2,1)}, f32[8,2,16,1024]{3,2,1,0:T(8,128)}) custom-call(bf16[8,2,8]{2,1,0:T(2,128)(2,1)} %scales_ref.1, s32[16]{0:T(128)} %fork_ref.1, s32[8,32]{1,0:T(8,128)} %bitcast.1, s32[1]{0:T(128)S(6)} %copy.11.length_ref, bf16[8,2,16,1024]{3,2,1,0:T(8,128)(2,1)} %pages_hbm.1, ...), custom_call_target="tpu_custom_call" | custom-call | flops 1342177280 | bytes 4194304 | tf_op jit(solution)/shard_map/pallas_call | solution.py:440
  42.6 2.5 %shard_map.104 = (bf16[1,128,4096]{2,1,0:T(8,128)(2,1)}, bf16[2,1,128,512]{3,2,1,0:T(8,128)(2,1)}, f32[8,2,16,1024]{3,2,1,0:T(8,128)}) custom-call(bf16[1,128,4096]{2,1,0:T(8,128)(2,1)} %get-tuple-element.6.dq_in, bf16[2,1,128,512]{3,2,1,0:T(8,128)(2,1)} %get-tuple-element.7.dkv_in, f32[8,2,16,1024]{3,2,1,0:T(8,128)} %get-tuple-element.8.pool_in), custom_call_target="tpu_custom_call" | custom-call | tf_op jit(solution)/shard_map/pallas_call | solution.py:468

commit v6 on v4

--- a/solution.py
+++ b/solution.py
@@ -81,7 +81,6 @@
     arrived,
     back,
     returned,
-    summed,
     part_out,
     part_in,
     queries,
@@ -141,35 +140,6 @@
     for load in loads:
         load.start()
 
-    factors = []
-    for n in range(pool_dev):
-        pair = scales_ref[n].astype(F32)
-        for c in range(2):
-            factors.append(jnp.broadcast_to(pair[c : c + 1, :], (page_rows, mp * kv)))
-    factors = jnp.concatenate(factors, 0)
-    pages_load.wait()
-    for head in range(mp * kv):
-        lanes = slice(head * DH, (head + 1) * DH)
-        inner = slice(head % width * DH, (head % width + 1) * DH)
-        scaled = pages_ref[:, lanes].astype(F32) * factors[:, head : head + 1]
-        slab[head // width, :, inner] = scaled.astype(BF16)
-    pl.semaphore_wait(barrier, dp + mp - 2)
-
-    my_rows = pl.ds(pl.multiple_of(my_mp * store_rows, store_rows), store_rows)
-    for c in range(chunks):
-        for k in range(1, mp):
-            other = lax.rem(my_mp + k, mp)
-            pltpu.make_async_remote_copy(
-                src_ref=slab.at[other * chunks + c],
-                dst_ref=grouped.at[c, my_rows],
-                send_sem=mp_send.at[c],
-                recv_sem=mp_recv.at[c],
-                device_id={"mp": other},
-                device_id_type=MESH,
-            ).start()
-    for c in range(chunks):
-        grouped[c, my_rows] = slab[my_mp * chunks + c]
-
     iota = functools.partial(lax.broadcasted_iota, jnp.int32)
     ahead = iota((slot, pick.shape[1]), 1) - iota((slot, pick.shape[1]), 0)
 
@@ -184,6 +154,37 @@
             )
         codes[r] = code
         pick[pl.ds(pl.multiple_of(r * slot, slot), slot), :] = ones_where(ahead == code)
+
+    factors = []
+    for n in range(pool_dev):
+        pair = scales_ref[n].astype(F32)
+        for c in range(2):
+            factors.append(jnp.broadcast_to(pair[c : c + 1, :], (page_rows, mp * kv)))
+    factors = jnp.concatenate(factors, 0)
+    my_rows = pl.ds(pl.multiple_of(my_mp * store_rows, store_rows), store_rows)
+    pages_load.wait()
+    for c in range(chunks):
+        for m in range(mp):
+            for i in range(width):
+                head = m * kv + c * width + i
+                scaled = (
+                    pages_ref[:, head * DH : (head + 1) * DH].astype(F32)
+                    * factors[:, head : head + 1]
+                )
+                slab[m * chunks + c, :, i * DH : (i + 1) * DH] = scaled.astype(BF16)
+        if c == 0:
+            pl.semaphore_wait(barrier, dp + mp - 2)
+        for k in range(1, mp):
+            other = lax.rem(my_mp + k, mp)
+            pltpu.make_async_remote_copy(
+                src_ref=slab.at[other * chunks + c],
+                dst_ref=grouped.at[c, my_rows],
+                send_sem=mp_send.at[c],
+                recv_sem=mp_recv.at[c],
+                device_id={"mp": other},
+                device_id_type=MESH,
+            ).start()
+        grouped[c, my_rows] = slab[my_mp * chunks + c]
 
     def select(out_ref, matrix, operand):
         def body(start, size):
@@ -326,13 +327,27 @@
     def column(m, c):
         return pl.ds(pl.multiple_of((m * chunks + c) * span, span), span)
 
+    def settled(m, c, block):
+        at = (slice(None), column(m, c))
+        pool_buf[at] = block
+        pltpu.make_async_copy(pool_buf.at[at], pool_hbm.at[at], out_sem.at[2]).start()
+
+    def finish(c):
+        if mp > 1:
+            wait_bytes(part_in.at[c, pl.ds(0, mp - 1)], fm_recv.at[c])
+        for k in range(1, mp):
+            other = lax.rem(my_mp + k, mp)
+            settled(other, c, part_in[c, other].astype(F32))
+
+    def summed(m, c):
+        rows = pl.ds(pl.multiple_of(m * store_rows, store_rows), store_rows)
+        return jnp.dot(pick_t[rows, :], returned[c], preferred_element_type=F32)
+
     for c in range(chunks):
         wait_bytes(returned.at[c, dp_rows], rt_recv.at[c])
-        select(summed, pick_t, returned[c])
         for k in range(1, mp):
             other = lax.rem(my_mp + k, mp)
-            rows = pl.ds(pl.multiple_of(other * store_rows, store_rows), store_rows)
-            part_out[other * chunks + c] = summed[rows, :].astype(BF16)
+            part_out[other * chunks + c] = summed(other, c).astype(BF16)
             pltpu.make_async_remote_copy(
                 src_ref=part_out.at[other * chunks + c],
                 dst_ref=part_in.at[c, my_mp],
@@ -341,15 +356,10 @@
                 device_id={"mp": other},
                 device_id_type=MESH,
             ).start()
-        pool_buf[:, column(my_mp, c)] = summed[my_rows, :]
-    for c in range(chunks):
-        if mp > 1:
-            wait_bytes(part_in.at[c, pl.ds(0, mp - 1)], fm_recv.at[c])
-        for k in range(1, mp):
-            other = lax.rem(my_mp + k, mp)
-            pool_buf[:, column(other, c)] = part_in[c, other].astype(F32)
-    last = pltpu.make_async_copy(pool_buf, pool_hbm, out_sem.at[2])
-    last.start()
+        settled(my_mp, c, summed(my_mp, c))
+        if c > 0:
+            finish(c - 1)
+    finish(chunks - 1)
     for c in range(chunks):
         if mp > 1:
             wait_bytes(grouped.at[c, mp_rows], mp_send.at[c])
@@ -358,7 +368,7 @@
         wait_bytes(returned.at[c, dp_rows], rt_send.at[c])
     for store in stores:
         store.wait()
-    last.wait()
+    pltpu.make_async_copy(pool_buf, pool_hbm, out_sem.at[2]).wait()
 
 
 def settle(dq_in, dkv_in, pool_in, dq_out, dkv_out, pool_out, dq_buf, dkv_buf, pool_buf, sem):
@@ -430,7 +440,6 @@
         ((chunks, slots, span), BF16),
         ((chunks, slots, span), BF16),
         ((chunks, slots, span), BF16),
-        ((group_rows, span), F32),
         ((mp * chunks, store_rows, span), BF16),
         ((chunks, mp, store_rows, span), BF16),
         ((kv, group * resp_len, DH), BF16),

time: 43.3 us -> 42.8 us (0.988)
  Pallas kernels: 41.8 us -> 41.2 us
    pallas_call x1, Pallas kernels: 39.3 us -> 38.7 us  [per_device(): pl.pallas_call(functools.partial(kernel, dp, mp, kv, group, width), out_s...]
where the time goes in v6:
time: 42.8 us; the launch traced here: 42.5 us
  Pallas kernels  41.2 us (96%)
  between operations  1.29 us (3%)
    pallas_call x1, Pallas kernels, per_device(): pl.pallas_call(functools.partial(kernel, dp, mp, kv, group, width), out_s...  38.7 us
    pallas_call x1, Pallas kernels, per_device(): pl.pallas_call(settle, out_shape=out_shape, in_specs=[hbm] * 3, out_specs...  2.5 us

profile of v6, /device:TPU:0, one launch (start us, length us, event | category | flops | bytes accessed | tf_op | source)
XLA Modules:
  0.0 42.5 jit_solution(15390830149169553609)
XLA Ops:
  1.3 38.7 %shard_map.103 = (bf16[1,128,4096]{2,1,0:T(8,128)(2,1)}, bf16[2,1,128,512]{3,2,1,0:T(8,128)(2,1)}, f32[256,1024]{1,0:T(8,128)}) custom-call(bf16[8,2,8]{2,1,0:T(2,128)(2,1)} %scales_ref.1, s32[16]{0:T(128)} %fork_ref.1, s32[8,32]{1,0:T(8,128)} %bitcast.5, s32[1]{0:T(128)S(6)} %copy.11.length_ref, bf16[256,1024]{1,0:T(8,128)(2,1)} %bitcast.4, ...), custom_call_target="tpu_custom_call" | custom-call | flops 1342177280 | bytes 4194304 | tf_op jit(solution)/shard_map/pallas_call | solution.py:452
  40.0 2.5 %shard_map.104 = (bf16[1,128,4096]{2,1,0:T(8,128)(2,1)}, bf16[2,1,128,512]{3,2,1,0:T(8,128)(2,1)}, f32[256,1024]{1,0:T(8,128)}) custom-call(bf16[1,128,4096]{2,1,0:T(8,128)(2,1)} %get-tuple-element.9.dq_in, bf16[2,1,128,512]{3,2,1,0:T(8,128)(2,1)} %get-tuple-element.10.dkv_in, f32[256,1024]{1,0:T(8,128)} %get-tuple-element.11.pool_in), custom_call_target="tpu_custom_call" | custom-call | tf_op jit(solution)/shard_map/pallas_call | solution.py:480
